TPU v7x, 128 devices: a whole 4x4x4 slice. The times are simulated.
128 devices in a mesh: ctx: 8 (over x, core), grp: 16 (over y, z).
Axes of the slice: x: 4, y: 4, z: 4, core: 2. Of those that a mesh axis runs over, the one named last changes fastest.
Arguments:
- queries: float32 [16, 2048, 16, 128], P('grp', 'ctx'), may hold values from -6 to 6
- key_vecs: float32 [16, 2048, 16, 128], P('grp', 'ctx'), may hold values from -6 to 6
- val_vecs: float32 [16, 2048, 32, 128], P('grp', 'ctx'), may hold values from -6 to 6
- out_gate: float32 [16, 2048, 32, 128], P('grp', 'ctx'), may hold values from -6 to 6
- log_decay: float32 [16, 32, 2048], P('grp', None, 'ctx'), may hold values from -0.8 to 0
- beta_gate: float32 [16, 32, 2048], P('grp', None, 'ctx'), may hold values from 0.1 to 0.9
- norm_gain: float32 [128], replicated, may hold values from 0.25 to 1.75
- lengths: int32 [16, 4], P('grp'), may hold values from 1 to 1024, 2048 in all within a row
- owner_slot: int32 [64], replicated, may hold values from 0 to 63, each once
Outputs:
- attn_out: float32 [16, 2048, 32, 128], P('grp', 'ctx')
- decode_states: float32 [64, 32, 128, 128], P('grp', 'ctx')
Inputs may be any that keep to these rules, and one draw needn't show every extreme that they name: Each group's 4 prompt lengths sum to 2048; the longest is exactly 1024. `owner_slot`: a permutation of the 64 decode slots.
All inputs are finite; a program needn't handle non-finite values.
Results may differ from a plain program's by a relative error of at most 0.0003.
Values sent between devices are 32-bit elements; how exact they have to be, the bound alone decides.
A program may use at most 256 MiB of HBM per device.

v0:
```python
import jax
import jax.numpy as jnp
from jax import lax
from jax.sharding import PartitionSpec as P

DK = 128
CH = 64


exact_mode = lax.Precision.HIGHEST


def shifted(block, axis, distance):
    devices = range(lax.axis_size(axis))
    route = [(i - distance, i) for i in devices if i - distance in devices]
    return lax.ppermute(block, axis, route)


def unit_norm(vectors):
    return vectors / jnp.sqrt(jnp.sum(vectors * vectors, axis=-1, keepdims=True) + 1e-06)


def batch_mm(left_mat, right_mat):
    return jnp.einsum("...ij,...jk->...ik", left_mat, right_mat, precision=exact_mode)


def span_terms(query_blk, key_blk, value_blk, decay_blk, beta_blk, segment_blk, carry_mask):
    block_len = query_blk.shape[-2]
    key_dim = key_blk.shape[-1]
    value_dim = value_blk.shape[-1]
    cumlog = jnp.cumsum(decay_blk, axis=-1)
    log_diffs = cumlog[..., :, None] - cumlog[..., None, :]
    row_ids = lax.broadcasted_iota(jnp.int32, (block_len, block_len), 0)
    col_ids = lax.broadcasted_iota(jnp.int32, (block_len, block_len), 1)
    same_seg = segment_blk[..., :, None] == segment_blk[..., None, :]
    inclusive = same_seg & (col_ids <= row_ids)
    strictly = same_seg & (col_ids < row_ids)
    decay_in = jnp.where(inclusive, jnp.exp(jnp.where(inclusive, log_diffs, 0.0)), 0.0)
    decay_st = jnp.where(strictly, decay_in, 0.0)
    key_gram = jnp.einsum("...id,...jd->...ij", key_blk, key_blk, precision=exact_mode)
    lower_part = beta_blk[..., :, None] * key_gram * decay_st
    identity = jnp.eye(block_len, dtype=jnp.float32)
    gamma_vec = jnp.exp(cumlog) * carry_mask
    rhs_all = jnp.concatenate(
        [beta_blk[..., None] * value_blk, (beta_blk * gamma_vec)[..., None] * key_blk], axis=-1
    )
    system_mat = identity + lower_part
    solved = lax.linalg.triangular_solve(
        system_mat, rhs_all, left_side=True, lower=True, unit_diagonal=True
    )
    upd_base = solved[..., :value_dim]
    write_keys = solved[..., value_dim:]
    scores = jnp.einsum("...id,...jd->...ij", query_blk, key_blk, precision=exact_mode) * decay_in
    out_base = batch_mm(scores, upd_base)
    query_eff = gamma_vec[..., None] * query_blk - batch_mm(scores, write_keys)
    tail_keys = decay_in[..., -1, :][..., None] * key_blk
    eye_key = jnp.eye(key_dim, dtype=jnp.float32)
    transition = gamma_vec[..., -1][..., None, None] * eye_key - jnp.einsum(
        "...jd,...je->...de", write_keys, tail_keys, precision=exact_mode
    )
    bias_term = jnp.einsum("...jv,...jd->...vd", upd_base, tail_keys, precision=exact_mode)
    return (out_base, query_eff, write_keys, upd_base, transition, bias_term, decay_in, gamma_vec)


def compose(earlier_pair, later_pair):
    return (
        batch_mm(earlier_pair[0], later_pair[0]),
        batch_mm(earlier_pair[1], later_pair[0]) + later_pair[1],
    )


def slab_terms(
    query_src, key_src, value_src, decay_src, beta_src, seq_ends, seq_starts, offset_pos
):
    tok_count = query_src.shape[0]
    head_count = value_src.shape[1]
    group_rep = head_count // query_src.shape[1]
    block_count = tok_count // CH
    positions = offset_pos + jnp.arange(tok_count, dtype=jnp.int32)
    segment = jnp.sum((positions[:, None] >= seq_ends[None, :]).astype(jnp.int32), axis=1)
    is_first = jnp.sum((positions[:, None] == seq_starts[None, :]).astype(jnp.int32), axis=1)
    segment_blk = segment.reshape(block_count, 1, CH)
    carry_mask = (jnp.cumsum(is_first.reshape(block_count, CH), axis=1) == 0).astype(jnp.float32)[
        :, None, :
    ]

    def to_blocks(source_arr):
        return source_arr.reshape(block_count, CH, head_count, source_arr.shape[-1]).transpose(
            0, 2, 1, 3
        )

    query_blk = to_blocks(jnp.repeat(unit_norm(query_src) * DK ** (-0.5), group_rep, axis=1))
    key_blk = to_blocks(jnp.repeat(unit_norm(key_src), group_rep, axis=1))
    value_blk = to_blocks(value_src)
    decay_blk = decay_src.reshape(head_count, block_count, CH).transpose(1, 0, 2)
    beta_blk = beta_src.reshape(head_count, block_count, CH).transpose(1, 0, 2)
    terms = span_terms(query_blk, key_blk, value_blk, decay_blk, beta_blk, segment_blk, carry_mask)
    return (key_blk, terms)


def run_blocks(incoming, terms, key_blk, seq_ends, offset_pos):
    out_base, query_eff, write_keys, upd_base, transition, bias_term, decay_in, gamma_vec = terms
    block_count = key_blk.shape[0]
    head_count = key_blk.shape[1]
    tok_count = block_count * CH
    req_count = seq_ends.shape[0]
    value_dim = upd_base.shape[-1]

    def advance(run_state, block_item):
        out_b, query_e, write_k, upd_b, trans_b, bias_b = block_item
        out_blk = out_b + jnp.einsum("hid,hvd->hiv", query_e, run_state, precision=exact_mode)
        upd_blk = upd_b - jnp.einsum("hid,hvd->hiv", write_k, run_state, precision=exact_mode)
        return (batch_mm(run_state, trans_b) + bias_b, (out_blk, upd_blk, run_state))

    _, (out_all, upd_all, start_all) = lax.scan(
        advance, incoming, (out_base, query_eff, write_keys, upd_base, transition, bias_term)
    )
    local_end = seq_ends - 1 - offset_pos
    end_pick = (
        (local_end[:, None] == jnp.arange(tok_count, dtype=jnp.int32)[None, :])
        .astype(jnp.float32)
        .reshape(req_count, block_count, CH)
    )
    weights = jnp.einsum("rni,nhij->nhrj", end_pick, decay_in, precision=exact_mode)
    amplitude = jnp.einsum("rni,nhi->rh", end_pick, gamma_vec, precision=exact_mode)
    start_part = jnp.einsum(
        "rn,nhvd->rhvd", jnp.sum(end_pick, axis=2), start_all, precision=exact_mode
    )
    weighted = weights[..., None] * upd_all[:, :, None, :, :]
    end_buf = amplitude[..., None, None] * start_part + jnp.einsum(
        "nhrjv,nhjd->rhvd", weighted, key_blk, precision=exact_mode
    )
    raw_out = out_all.transpose(0, 2, 1, 3).reshape(tok_count, head_count, value_dim)
    return (raw_out, end_buf)


def local(
    queries, key_vecs, val_vecs, out_gate, log_decay, beta_gate, norm_gain, lengths, owner_slot
):
    ctx_count = lax.axis_size("ctx")
    tok_count = queries.shape[1]
    req_count = lengths.shape[1]
    seq_ends = jnp.cumsum(lengths[0])
    seq_starts = seq_ends - lengths[0]
    offset_pos = lax.axis_index("ctx") * tok_count
    key_blk, terms = slab_terms(
        queries[0],
        key_vecs[0],
        val_vecs[0],
        log_decay[0],
        beta_gate[0],
        seq_ends,
        seq_starts,
        offset_pos,
    )
    head_count = key_blk.shape[1]
    key_dim = key_blk.shape[-1]
    value_dim = terms[3].shape[-1]
    eye_heads = jnp.broadcast_to(
        jnp.eye(key_dim, dtype=jnp.float32), (head_count, key_dim, key_dim)
    )
    zero_state = jnp.zeros((head_count, value_dim, key_dim), jnp.float32)

    def fold_block(acc_pair, block_pair):
        return (compose(acc_pair, block_pair), None)

    (slab_trans, slab_bias), _ = lax.scan(fold_block, (eye_heads, zero_state), (terms[4], terms[5]))

    def pass_state(step_idx, run_state):
        next_state = batch_mm(run_state, slab_trans) + slab_bias
        return shifted(next_state, "ctx", 1)

    incoming = lax.fori_loop(0, ctx_count - 1, pass_state, zero_state)
    raw_out, end_buf = run_blocks(incoming, terms, key_blk, seq_ends, offset_pos)
    own_states = lax.psum_scatter(end_buf, "ctx", scatter_dimension=1, tiled=True)
    slot_base = lax.axis_index("grp") * req_count
    route_mat = (
        owner_slot[None, :] == slot_base + jnp.arange(req_count, dtype=jnp.int32)[:, None]
    ).astype(jnp.float32)
    decode_states = jnp.einsum(
        "pi,ihvd->phvd",
        route_mat,
        lax.all_gather(own_states, "grp", axis=0, tiled=True),
        precision=exact_mode,
    )
    mean_sq = jnp.mean(raw_out * raw_out, axis=-1, keepdims=True)
    attn_out = raw_out / jnp.sqrt(mean_sq + 1e-06) * norm_gain * jax.nn.silu(out_gate[0])
    return (attn_out[None], decode_states)


def solution(mesh):
    return jax.shard_map(
        local,
        mesh=mesh,
        in_specs=(
            P("grp", "ctx", None, None),
            P("grp", "ctx", None, None),
            P("grp", "ctx", None, None),
            P("grp", "ctx", None, None),
            P("grp", None, "ctx"),
            P("grp", None, "ctx"),
            P(),
            P("grp", None),
            P(),
        ),
        out_specs=(P("grp", "ctx", None, None), P("grp", "ctx", None, None)),
        check_vma=False,
    )
```

profile of v0, /device:TPU:5, one launch (start us, length us, event | category | flops | bytes accessed | tf_op | source)
XLA Modules:
  0.0 1286.3 jit_solution(6889322097711782732)
XLA Ops:
  20.6 8.1 fusion.52
  31.1 8.2 fusion.48
  53.4 12.3 fusion.45
  68.9 7.3 copy.276
  83.4 265.1 %custom-call.3 = f32[4,32,1,64,64]{1,3,4,2,0:T(8,128)} custom-call(f32[4,32,1,64,64]{1,4,3,2,0:T(8,128)} %get-tuple-element.336), custom_call_target="InvertDiagBlocksLowerTriangular" | custom-call | tf_op jit(solution)/shard_map/triangular_solve | solution.py:48
  348.5 8.7 copy.256
  357.2 8.6 bitcast_multiply_fusion.1
  365.8 11.6 fusion.39
  398.7 19.0 %fusion.54 = f32[4,32,128,128]{2,3,1,0:T(8,128)} fusion(f32[4,64,32,128]{3,1,0,2:T(8,128)} %bitcast.199, f32[4,32,64]{2,1,0:T(8,128)S(1)} %copy.257, f32[4,32,64,256]{3,2,1,0:T(8,128)} %copy-done.3), kind=kOutput, calls=%fused_computation.61 | convolution fusion | flops 1611661312 | bytes 16809984 | tf_op jit(solution)/shard_map/...jv,...jd->...vd/dot_general | solution.py:61
  417.7 18.3 %multiply_subtract_fusion = f32[4,32,128,128]{3,2,1,0:T(8,128)} fusion(f32[128,128]{1,0:T(8,128)S(1)} %fusion.69, f32[4,32]{1,0:T(4,128)S(1)} %slice_reduce_fusion, f32[4,64,32,128]{3,1,0,2:T(8,128)S(1)} %bitcast.201, f32[4,32,64]{2,1,0:T(8,128)S(1)} %copy.257, f32[4,32,64,256]{3,2,1,0:T(8,128)S(1)} %copy-done.4), kind=kOutput, calls=%fused_computation.45 | convolution fusion | flops 1615855616 | bytes 16910336 | tf_op jit(solution)/shard_map/...jd,...je->...de/dot_general | solution.py:58
  436.0 8.9 copy.258
  445.2 43.2 %while.41 = (s32[]{:T(128)}, f32[32,128,128]{1,2,0:T(8,128)S(1)}, f32[32,128,128]{1,2,0:T(8,128)}, f32[4,32,128,128]{2,3,1,0:T(8,128)}, f32[4,32,128,128]{2,3,1,0:T(8,128)}, /*index=5*/s32[]{:T(128)}, s32[]{:T(128)}) while((s32[]{:T(128)}, f32[32,128,128]{1,2,0:T(8,128)S(1)}, f32[32,128,128]{1,2,0:T(8,128)}, ...), condition=%wide.region_7.8_spmd.clone, body=%wide.region_6.7_spmd.clone.sunk | while | flops 1611661312 | bytes 56624764 | solution.py:167
  493.4 232.0 %while.39 = (s32[]{:T(128)}, f32[32,128,128]{2,1,0:T(8,128)S(1)}, f32[32,128,128]{2,1,0:T(8,128)}, f32[32,128,128]{2,1,0:T(8,128)}, s32[]{:T(128)}) while((s32[]{:T(128)}, f32[32,128,128]{2,1,0:T(8,128)S(1)}, f32[32,128,128]{2,1,0:T(8,128)}, f32[32,128,128]{2,1,0:T(8,128)}, s32[]{:T(128)}) %tuple.92), condition=%wide.region_9.10_spmd, body=%wide.region_8.9_spmd.sunk | while | flops 805830656 | bytes 16777316 | solution.py:173
  502.5 23.3 %collective-permute-done = f32[32,128,128]{2,1,0:T(8,128)S(1)} collective-permute-done((f32[32,128,128]{2,1,0:T(8,128)}, f32[32,128,128]{2,1,0:T(8,128)S(1)}, u32[]{:S(2)}, u32[]{:S(2)}) %collective-permute-start) | collective-permute-done | bytes 2097184 | tf_op jit(solution)/shard_map/while/body/eval_jaxpr/ppermute | solution.py:16
  535.8 23.3 %collective-permute-done = f32[32,128,128]{2,1,0:T(8,128)S(1)} collective-permute-done((f32[32,128,128]{2,1,0:T(8,128)}, f32[32,128,128]{2,1,0:T(8,128)S(1)}, u32[]{:S(2)}, u32[]{:S(2)}) %collective-permute-start) | collective-permute-done | bytes 2097184 | tf_op jit(solution)/shard_map/while/body/eval_jaxpr/ppermute | solution.py:16
  569.1 23.3 %collective-permute-done = f32[32,128,128]{2,1,0:T(8,128)S(1)} collective-permute-done((f32[32,128,128]{2,1,0:T(8,128)}, f32[32,128,128]{2,1,0:T(8,128)S(1)}, u32[]{:S(2)}, u32[]{:S(2)}) %collective-permute-start) | collective-permute-done | bytes 2097184 | tf_op jit(solution)/shard_map/while/body/eval_jaxpr/ppermute | solution.py:16
  602.4 23.3 %collective-permute-done = f32[32,128,128]{2,1,0:T(8,128)S(1)} collective-permute-done((f32[32,128,128]{2,1,0:T(8,128)}, f32[32,128,128]{2,1,0:T(8,128)S(1)}, u32[]{:S(2)}, u32[]{:S(2)}) %collective-permute-start) | collective-permute-done | bytes 2097184 | tf_op jit(solution)/shard_map/while/body/eval_jaxpr/ppermute | solution.py:16
  635.6 23.3 %collective-permute-done = f32[32,128,128]{2,1,0:T(8,128)S(1)} collective-permute-done((f32[32,128,128]{2,1,0:T(8,128)}, f32[32,128,128]{2,1,0:T(8,128)S(1)}, u32[]{:S(2)}, u32[]{:S(2)}) %collective-permute-start) | collective-permute-done | bytes 2097184 | tf_op jit(solution)/shard_map/while/body/eval_jaxpr/ppermute | solution.py:16
  668.9 23.3 %collective-permute-done = f32[32,128,128]{2,1,0:T(8,128)S(1)} collective-permute-done((f32[32,128,128]{2,1,0:T(8,128)}, f32[32,128,128]{2,1,0:T(8,128)S(1)}, u32[]{:S(2)}, u32[]{:S(2)}) %collective-permute-start) | collective-permute-done | bytes 2097184 | tf_op jit(solution)/shard_map/while/body/eval_jaxpr/ppermute | solution.py:16
  702.2 23.3 %collective-permute-done = f32[32,128,128]{2,1,0:T(8,128)S(1)} collective-permute-done((f32[32,128,128]{2,1,0:T(8,128)}, f32[32,128,128]{2,1,0:T(8,128)S(1)}, u32[]{:S(2)}, u32[]{:S(2)}) %collective-permute-start) | collective-permute-done | bytes 2097184 | tf_op jit(solution)/shard_map/while/body/eval_jaxpr/ppermute | solution.py:16
  727.3 302.9 %while.40 = (s32[]{:T(128)}, f32[32,128,128]{1,2,0:T(8,128)}, f32[4,32,64,128]{3,2,1,0:T(8,128)}, f32[4,32,64,128]{3,2,0,1:T(8,128)}, f32[4,32,128,128]{3,0,2,1:...) while((s32[]{:T(128)}, f32[32,128,128]{1,2,0:T(8,128)}, ...), condition=%wide.region_12.13_spmd, body=%wide.region_11.12_spmd.sunk | while | flops 1611661312 | bytes 31460488 | solution.py:115
  748.2 55.1 %dynamic_update_slice.18 = f32[4,32,128,128]{3,0,2,1:T(4,128)} dynamic-update-slice(f32[4,32,128,128]{3,0,2,1:T(4,128)} %get-tuple-element.522, f32[1,32,128,128]{3,0,2,1:T(1,128)} %copy.344, s32[]{:T(128)S(6)} %copy.368, s32[]{:T(128)} %constant.67.clone.1..sunk, s32[]{:T(128)} %constant.67.clone.1..sunk, s32[]{:T(128)} %constant.67.clone.1..sunk) | dynamic-update-slice | bytes 4194308 | tf_op jit(solution)/shard_map/while/body/jit(dynamic_update_index_in_dim)/dynamic_update_slice | solution.py:115
  823.8 55.1 %dynamic_update_slice.18 = f32[4,32,128,128]{3,0,2,1:T(4,128)} dynamic-update-slice(f32[4,32,128,128]{3,0,2,1:T(4,128)} %get-tuple-element.522, f32[1,32,128,128]{3,0,2,1:T(1,128)} %copy.344, s32[]{:T(128)S(6)} %copy.368, s32[]{:T(128)} %constant.67.clone.1..sunk, s32[]{:T(128)} %constant.67.clone.1..sunk, s32[]{:T(128)} %constant.67.clone.1..sunk) | dynamic-update-slice | bytes 4194308 | tf_op jit(solution)/shard_map/while/body/jit(dynamic_update_index_in_dim)/dynamic_update_slice | solution.py:115
  899.5 55.1 %dynamic_update_slice.18 = f32[4,32,128,128]{3,0,2,1:T(4,128)} dynamic-update-slice(f32[4,32,128,128]{3,0,2,1:T(4,128)} %get-tuple-element.522, f32[1,32,128,128]{3,0,2,1:T(1,128)} %copy.344, s32[]{:T(128)S(6)} %copy.368, s32[]{:T(128)} %constant.67.clone.1..sunk, s32[]{:T(128)} %constant.67.clone.1..sunk, s32[]{:T(128)} %constant.67.clone.1..sunk) | dynamic-update-slice | bytes 4194308 | tf_op jit(solution)/shard_map/while/body/jit(dynamic_update_index_in_dim)/dynamic_update_slice | solution.py:115
  975.1 55.1 %dynamic_update_slice.18 = f32[4,32,128,128]{3,0,2,1:T(4,128)} dynamic-update-slice(f32[4,32,128,128]{3,0,2,1:T(4,128)} %get-tuple-element.522, f32[1,32,128,128]{3,0,2,1:T(1,128)} %copy.344, s32[]{:T(128)S(6)} %copy.368, s32[]{:T(128)} %constant.67.clone.1..sunk, s32[]{:T(128)} %constant.67.clone.1..sunk, s32[]{:T(128)} %constant.67.clone.1..sunk) | dynamic-update-slice | bytes 4194308 | tf_op jit(solution)/shard_map/while/body/jit(dynamic_update_index_in_dim)/dynamic_update_slice | solution.py:115
  1030.2 22.2 %fusion.57 = f32[32,128,4,128]{3,1,2,0:T(8,128)} fusion(f32[4,32,64,128,1]{3,2,0,4,1:T(8,128)} %bitcast.200, f32[4,32,64,128]{3,2,0,1:T(8,128)} %get-tuple-element.116, f32[4,32,4,64]{3,0,2,1:T(4,128)S(1)} %copy.277), kind=kOutput, calls=%fused_computation.64 | convolution fusion | flops 6446645248 | bytes 16908288 | tf_op jit(solution)/shard_map/nhrjv,nhjd->rhvd/dot_general | solution.py:130
  1052.4 9.9 copy.280
  1062.3 21.9 %bitcast_add_fusion.2 = f32[4,32,128,128]{3,0,2,1:T(4,128)S(1)} fusion(f32[32,128,4,128]{1,2,3,0:T(4,128)} %copy.280, f32[4,32,128,128]{3,0,2,1:T(4,128)} %get-tuple-element.115, f32[4,32]{0,1:T(8,128)S(1)} %copy-done.11, f32[4,4]{0,1:T(4,128)S(1)} %copy-done.12), kind=kOutput, calls=%fused_computation.40 | convolution fusion | flops 104857600 | bytes 25166400 | tf_op jit(solution)/shard_map/rn,nhvd->rhvd/dot_general | solution.py:126
  1088.7 54.6 %reduce-scatter.2.cloned.1.call-done = f32[4,4,128,128]{3,2,0,1:T(8,128)} async-done(((f32[4,32,128,128]{3,2,0,1:T(8,128)}), f32[4,4,128,128]{3,2,0,1:T(8,128)}) %reduce-scatter.2.cloned.1.call-update) | async-done | bytes 1048592 | tf_op jit(solution)/shard_map/reduce_scatter | solution.py:175
  1155.8 7.8 fusion.47
  1163.6 94.7 %all-gather.2.cloned.1.call-done = f32[64,4,128,128]{3,2,1,0:T(8,128)} async-done(((f32[4,4,128,128]{3,2,1,0:T(8,128)}), f32[64,4,128,128]{3,2,1,0:T(8,128)}) %all-gather.2.cloned.1.call-update) | async-done | bytes 16777232 | tf_op jit(solution)/shard_map/all_gather | solution.py:183
  1258.3 19.8 %fusion.35 = f32[4,4,128,128]{3,0,2,1:T(4,128)S(1)} fusion(f32[64,4,128,128]{3,2,1,0:T(8,128)} %all-gather.2.cloned.1.call-done, s32[64]{0:T(128)S(1)} %copy-done.14, s32[4]{0:T(128)S(1)} %iota_add_fusion.1), kind=kOutput, calls=%fused_computation.32 | convolution fusion | flops 201326848 | bytes 17826064 | tf_op jit(solution)/shard_map/pi,ihvd->phvd/dot_general | solution.py:180
  (155 shorter events, 280.7 us)
Async XLA Ops:
  7.2 9.2 copy-start.9
  7.2 1136.2 %reduce-scatter.2.cloned.1.call-start = ((), (), s32[]{:S(2)}) async-start(), calls=%async_computation.1 | async-start | bytes 9437184 | tf_op jit(solution)/shard_map/reduce_scatter | solution.py:175
  17.1 1.6 copy-start.10
  20.6 8.6 copy-start
  29.2 2.0 copy-start.6
  65.7 3.2 copy-start.8
  365.8 11.6 copy-start.5
  365.8 11.6 copy-start.7
  377.4 12.9 %copy-start.3 = (f32[4,32,64,256]{3,2,1,0:T(8,128)}, f32[4,32,64,256]{3,2,1,0:T(8,128)S(1)}, u32[]{:S(2)}) copy-start(f32[4,32,64,256]{3,2,1,0:T(8,128)S(1)} %fusion.39) | copy-start | bytes 25165828
  398.7 19.0 %copy-start.1 = (f32[256,16,2,128]{3,0,2,1:T(8,128)S(1)}, f32[256,16,2,128]{3,0,2,1:T(8,128)}, u32[]{:S(2)}) copy-start(f32[256,16,2,128]{3,0,2,1:T(8,128)} %copy-done) | copy-start | bytes 12582916
  398.7 19.0 %copy-start.4 = (f32[4,32,64,256]{3,2,1,0:T(8,128)S(1)}, f32[4,32,64,256]{3,2,1,0:T(8,128)}, u32[]{:S(2)}) copy-start(f32[4,32,64,256]{3,2,1,0:T(8,128)} %copy-done.3) | copy-start | bytes 25165828
  445.2 4.0 copy-start.2
  456.0 4.0 copy-start.2
  466.8 4.0 copy-start.2
  477.6 4.0 copy-start.2
  499.2 26.7 %collective-permute-start = (f32[32,128,128]{2,1,0:T(8,128)}, f32[32,128,128]{2,1,0:T(8,128)S(1)}, u32[]{:S(2)}, u32[]{:S(2)}) collective-permute-start(f32[32,128,128]{2,1,0:T(8,128)} %convolution_add_fusion.3), channel_id=1, source_target_pairs={{0,16},{16,32},{32,48},{48,64},{64,80},{80,96},{96,112},{1,17},{17... | collective-permute-start | bytes 6291464 | tf_op jit(solution)/shard_map/while/body/eval_jaxpr/ppermute | solution.py:16
  531.5 27.6 %collective-permute-start = (f32[32,128,128]{2,1,0:T(8,128)}, f32[32,128,128]{2,1,0:T(8,128)S(1)}, u32[]{:S(2)}, u32[]{:S(2)}) collective-permute-start(f32[32,128,128]{2,1,0:T(8,128)} %convolution_add_fusion.3), channel_id=1, source_target_pairs={{0,16},{16,32},{32,48},{48,64},{64,80},{80,96},{96,112},{1,17},{17... | collective-permute-start | bytes 6291464 | tf_op jit(solution)/shard_map/while/body/eval_jaxpr/ppermute | solution.py:16
  564.8 27.6 %collective-permute-start = (f32[32,128,128]{2,1,0:T(8,128)}, f32[32,128,128]{2,1,0:T(8,128)S(1)}, u32[]{:S(2)}, u32[]{:S(2)}) collective-permute-start(f32[32,128,128]{2,1,0:T(8,128)} %convolution_add_fusion.3), channel_id=1, source_target_pairs={{0,16},{16,32},{32,48},{48,64},{64,80},{80,96},{96,112},{1,17},{17... | collective-permute-start | bytes 6291464 | tf_op jit(solution)/shard_map/while/body/eval_jaxpr/ppermute | solution.py:16
  598.1 27.6 %collective-permute-start = (f32[32,128,128]{2,1,0:T(8,128)}, f32[32,128,128]{2,1,0:T(8,128)S(1)}, u32[]{:S(2)}, u32[]{:S(2)}) collective-permute-start(f32[32,128,128]{2,1,0:T(8,128)} %convolution_add_fusion.3), channel_id=1, source_target_pairs={{0,16},{16,32},{32,48},{48,64},{64,80},{80,96},{96,112},{1,17},{17... | collective-permute-start | bytes 6291464 | tf_op jit(solution)/shard_map/while/body/eval_jaxpr/ppermute | solution.py:16
  631.3 27.6 %collective-permute-start = (f32[32,128,128]{2,1,0:T(8,128)}, f32[32,128,128]{2,1,0:T(8,128)S(1)}, u32[]{:S(2)}, u32[]{:S(2)}) collective-permute-start(f32[32,128,128]{2,1,0:T(8,128)} %convolution_add_fusion.3), channel_id=1, source_target_pairs={{0,16},{16,32},{32,48},{48,64},{64,80},{80,96},{96,112},{1,17},{17... | collective-permute-start | bytes 6291464 | tf_op jit(solution)/shard_map/while/body/eval_jaxpr/ppermute | solution.py:16
  664.6 27.6 %collective-permute-start = (f32[32,128,128]{2,1,0:T(8,128)}, f32[32,128,128]{2,1,0:T(8,128)S(1)}, u32[]{:S(2)}, u32[]{:S(2)}) collective-permute-start(f32[32,128,128]{2,1,0:T(8,128)} %convolution_add_fusion.3), channel_id=1, source_target_pairs={{0,16},{16,32},{32,48},{48,64},{64,80},{80,96},{96,112},{1,17},{17... | collective-permute-start | bytes 6291464 | tf_op jit(solution)/shard_map/while/body/eval_jaxpr/ppermute | solution.py:16
  697.9 27.6 %collective-permute-start = (f32[32,128,128]{2,1,0:T(8,128)}, f32[32,128,128]{2,1,0:T(8,128)S(1)}, u32[]{:S(2)}, u32[]{:S(2)}) collective-permute-start(f32[32,128,128]{2,1,0:T(8,128)} %convolution_add_fusion.3), channel_id=1, source_target_pairs={{0,16},{16,32},{32,48},{48,64},{64,80},{80,96},{96,112},{1,17},{17... | collective-permute-start | bytes 6291464 | tf_op jit(solution)/shard_map/while/body/eval_jaxpr/ppermute | solution.py:16
  1052.4 9.9 copy-start.11
  1052.4 9.9 copy-start.12
  1088.7 169.6 %all-gather.2.cloned.1.call-start = ((), (), s32[]{:S(2)}) async-start(), calls=%async_computation.2 | async-start | bytes 17825792 | tf_op jit(solution)/shard_map/all_gather | solution.py:183
  1149.1 6.7 copy-start.13
  1155.8 102.5 %copy-start.14 = (s32[64]{0:T(128)S(1)}, s32[64]{0:T(128)}, u32[]{:S(2)}) copy-start(s32[64]{0:T(128)} %param.23) | copy-start | bytes 772
Sparse Core Ops, SparseCore 0:
  1088.8 54.4 reduce-scatter.1
  1146.1 112.1 all-gather.1
where the time goes:
time: 1300 us; the launch traced here: 1290 us
  local copies, waits for them, and re-layouts  351 us (27%)
  waiting for transfers between devices  312 us (24%)
  other arithmetic  305 us (23%)
  matrix products  273 us (21%)
  starting transfers between devices  29.1 us (2%)
  between operations  14.7 us (1%)
    another operation x4, other arithmetic, span_terms(): lax.linalg.triangular_solve(system_mat, rhs_all, left_side=True, lower=Tr...  265 us
    dynamic_update_slice x8, local copies, waits for them, and re-layouts, run_blocks(): lax.scan(advance, incoming, (out_base, query_eff, write_keys, upd_base, t...  236 us
    ppermute x7, waiting for transfers between devices, shifted(): return lax.ppermute(block, axis, route)  163 us
    dot_general x21, matrix products, batch_mm(): jnp.einsum('...ij,...jk->...ik', left_mat, right_mat, precision=exact_mode)  103 us
    all_gather x1, waiting for transfers between devices, local(): lax.all_gather(own_states, 'grp', axis=0, tiled=True)  94.7 us
    reduce_scatter x1, waiting for transfers between devices, local(): lax.psum_scatter(end_buf, 'ctx', scatter_dimension=1, tiled=True)  54.6 us
    ppermute x7, starting transfers between devices, shifted(): return lax.ppermute(block, axis, route)  29 us
  transfers between devices with their start and end apart: 9, of which 9 were waited for; matrix products, arithmetic and copies ran while one was open for 1% of the time, Pallas kernels for 0%

commit v1 on v0

v1 whole, which is shorter than its diff:
```python
import jax
import jax.numpy as jnp
from jax import lax
from jax.experimental import pallas as pl
from jax.experimental.pallas import tpu as pltpu
from jax.sharding import PartitionSpec as P

CH = 64
D = 128
HK = 16
H = 32
TOK = 256
NC = TOK // CH
REQS = 4
F32 = jnp.float32
BF16 = jnp.bfloat16
MESH = pl.DeviceIdType.MESH
VMEM = pl.BlockSpec(memory_space=pltpu.VMEM)
SMEM = pl.BlockSpec(memory_space=pltpu.SMEM)


def mm(x, y):
    return lax.dot_general(x, y, (((1,), (0,)), ((), ())), preferred_element_type=F32)


def split(x):
    hi = x.astype(BF16)
    return hi, (x - hi.astype(F32)).astype(BF16)


def dot_wide(x, y):
    xh, xl = split(x)
    yh, yl = split(y)
    left = jnp.concatenate([xh, xl], axis=1)
    return mm(left, jnp.concatenate([yh, yh], axis=0)) + mm(xh, yl)


def dot_twin(x, y):
    low = x - x.astype(BF16).astype(F32)
    lane = lax.broadcasted_iota(jnp.int32, x.shape, 1)
    s = jnp.where(lane < CH, x, low).astype(BF16)
    yh, yl = split(y)
    left = jnp.concatenate([s, s], axis=1)
    return mm(left, jnp.concatenate([yh, yh, yl, yl], axis=0))


def prompt_ends(len_ref):
    ends = [len_ref[0, 0]]
    for r in range(1, REQS):
        ends.append(ends[-1] + len_ref[0, r])
    return ends


def seg_start(pos, ends):
    start = jnp.zeros(pos.shape, jnp.int32)
    for e in ends[:-1]:
        start = jnp.where(pos >= e, e, start)
    return start


def terms_kernel(
    len_ref, q_ref, k_ref, v_ref, ld_ref, be_ref,
    out0_ref, qe_ref, m1_ref, b1_ref, bo_ref, f0_ref, flag_ref,
    kn_s, qn_s, kt_s, gram_s, qk_s, low_s, inv_s, t_s,
    cum_s, gam_s, cumt_s, gamt_s, bet_s, start_s, bias_s, col_s, gcol_s, st_s, u_s,
):
    off = lax.axis_index("ctx") * TOK
    ends = prompt_ends(len_ref)
    lane = lax.broadcasted_iota(jnp.int32, (D, D), 1)
    row = lax.broadcasted_iota(jnp.int32, (D, D), 0)

    cum = ld_ref[...]
    tok = lane % CH
    for s in (1, 2, 4, 8, 16, 32):
        cum = cum + jnp.where(tok >= s, pltpu.roll(cum, s, 1), 0.0)
    lo_a = off + (row % NC) * CH
    carry_a = seg_start(lo_a + tok, ends) < lo_a
    gam = jnp.where(carry_a, jnp.exp(cum), 0.0)
    cum_s[...] = cum
    gam_s[...] = gam
    cumt_s[...] = cum.T[:CH]
    gamt_s[...] = gam.T[:CH]
    bet_s[...] = be_ref[...].T[:CH]
    lane_b = lane[:CH]
    row_b = row[:CH]
    start_s[...] = seg_start(off + (lane_b % NC) * CH + row_b, ends)
    tok_b = tok[:CH]
    for c in range(NC):
        lo = off + c * CH
        same = seg_start(lo + row_b, ends) == seg_start(lo + tok_b, ends)
        bias_s[pl.ds(c * CH, CH), :] = jnp.where(same & (tok_b <= row_b), 0.0, -1e30)

    @pl.loop(0, 8)
    def _(i):
        for u in range(16):
            f0_ref[i, u] = jnp.zeros((D, D), F32)

    @pl.loop(0, HK)
    def _(hk):
        k = k_ref[pl.ds(hk, TOK, stride=HK), :]
        q = q_ref[pl.ds(hk, TOK, stride=HK), :]
        kn = k * lax.rsqrt(jnp.sum(k * k, axis=1, keepdims=True) + 1e-6)
        qn = q * (lax.rsqrt(jnp.sum(q * q, axis=1, keepdims=True) + 1e-6) * (D**-0.5))
        kn_s[hk] = kn
        qn_s[hk] = qn
        for c in range(NC):
            kc = kn[c * CH : (c + 1) * CH]
            qc = qn[c * CH : (c + 1) * CH]
            kt = jnp.concatenate([kc, kc], axis=0).T
            kt_s[hk * NC + c] = kt
            g = dot_wide(jnp.concatenate([kc, qc], axis=0), kt)
            gram_s[pl.ds((hk * NC + c) * CH, CH), :] = g[:CH]
            qk_s[hk * NC + c] = g[CH:]

    @pl.loop(0, CH)
    def _(i):
        x = gram_s[pl.ds(i, HK * NC, stride=CH), :]
        xt = jnp.concatenate([x, x], axis=0).T[:CH]
        keep = (start_s[...] == start_s[pl.ds(i, 1), :]) & (row_b < i)
        decay = jnp.exp(jnp.where(keep, cumt_s[pl.ds(i, 1), :] - cumt_s[...], -1e30))
        low_s[pl.ds(i * CH, CH), :] = xt * decay * bet_s[pl.ds(i, 1), :]

    for g in range(CH // 4):
        n = 8 * ((4 * g + 3) // 8 + 1)
        rid = lax.broadcasted_iota(jnp.int32, (n, D), 0)
        acc = tuple(jnp.where(rid == 4 * g + a, 1.0, 0.0).astype(F32) for a in range(4))

        def body(jb, acc, g=g, n=n):
            acc = list(acc)
            for b in range(4):
                t = inv_s[pl.ds((jb * 4 + b) * CH, n), :]
                for a in range(4):
                    acc[a] = acc[a] - low_s[pl.ds((4 * g + a) * CH + jb * 4 + b, 1), :] * t
            return tuple(acc)

        if g:
            acc = lax.fori_loop(0, g, body, acc)
        acc = list(acc)
        for a in range(4):
            for b in range(a):
                acc[a] = acc[a] - low_s[pl.ds((4 * g + a) * CH + 4 * g + b, 1), :] * acc[b]
            inv_s[pl.ds((4 * g + a) * CH, n), :] = acc[a]
            if n < CH:
                inv_s[pl.ds((4 * g + a) * CH + n, CH - n), :] = jnp.zeros((CH - n, D), F32)

    @pl.loop(0, CH)
    def _(i):
        x = inv_s[pl.ds(i * CH, CH), :] * bet_s[...]
        t_s[pl.ds(i, D, stride=CH), :] = jnp.concatenate([x, x], axis=0).T

    first_end = ends[-1]
    for e in ends[-2::-1]:
        first_end = jnp.where(e > off, e, first_end)
    marks = [first_end >= off + TOK]
    begin = 0
    for e in ends:
        marks.append((begin <= off) & (e > off) & (e <= off + TOK))
        begin = e
    mark = jnp.zeros((8, D), F32)
    for i, m in enumerate(marks):
        mark = jnp.where(row[:8] == i, jnp.where(m, 1.0, 0.0), mark)
    flag_ref[...] = mark

    eye = jnp.where(lane == row, 1.0, 0.0).astype(F32)
    zero = jnp.zeros((CH, D), F32)

    @pl.loop(0, HK)
    def _(hk):
        shift = lax.rem(D - hk * NC, D)
        col_s[...] = pltpu.roll(cumt_s[...], shift, 1)
        gcol_s[...] = pltpu.roll(gamt_s[...], shift, 1)
        col = col_s[...]
        gcol = gcol_s[...]
        state = [jnp.concatenate([jnp.zeros((D, D), F32), eye], axis=1) for _ in range(2)]
        for c in range(NC):
            kc = kn_s[hk, pl.ds(c * CH, CH), :]
            qc = qn_s[hk, pl.ds(c * CH, CH), :]
            kt = kt_s[hk * NC + c]
            qk = qk_s[hk * NC + c]
            bias = bias_s[pl.ds(c * CH, CH), :]
            for r in range(2):
                at = r * CH + c
                b = r * CH + hk * NC + c
                ccol = col[:, at : at + 1]
                gc = gcol[:, at : at + 1]
                decay = jnp.exp(ccol - cum_s[pl.ds(b, 1), :] + bias)
                v = v_ref[pl.ds(c * CH * H + hk * 2 + r, CH, stride=H), :]
                gq = qc * gc
                uw = dot_twin(t_s[pl.ds(b * CH, CH), :], jnp.concatenate([v, kc * gc], axis=1))
                u0, w = uw[:, :D], uw[:, D:]
                if c == 0:
                    u = jnp.concatenate([u0, -w], axis=1)
                    base = jnp.concatenate([zero, gq], axis=1)
                else:
                    p = dot_wide(jnp.concatenate([w, gq], axis=0), state[r])
                    u = jnp.concatenate([u0, zero], axis=1) - p[:CH]
                    base = p[CH:]
                left = jnp.concatenate([qk * decay, kt * decay[CH - 1 : CH]], axis=0)
                res = dot_twin(left, u)
                o = base + res[:CH]
                h = hk * 2 + r
                out0_ref[h, pl.ds(c * CH, CH), :] = o[:, :D]
                qe_ref[h, pl.ds(c * CH, CH), :] = o[:, D:]
                st_s[r, c] = state[r]
                u_s[r, c] = u
                state[r] = gc[CH - 1 : CH] * state[r] + res[CH:]
        for r in range(2):
            h = hk * 2 + r
            bo_ref[h] = state[r][:, :D]
            b1_ref[h] = state[r][:, :D]
            m1_ref[h] = state[r][:, D:]
        begin = 0
        for p in range(REQS):
            last = ends[p] - 1 - off
            opens = begin <= off
            begin = ends[p]

            @pl.when((last >= 0) & (last < TOK))
            def _(last=last, opens=opens, p=p):
                c = last // CH
                e = last % CH
                for r in range(2):
                    h = hk * 2 + r
                    at = lane[:1] == r * CH + c
                    crow = cum_s[pl.ds(r * CH + hk * NC + c, 1), :]
                    cume = jnp.sum(jnp.where(at, col_s[pl.ds(e, 1), :], 0.0), axis=1, keepdims=True)
                    amp = jnp.sum(jnp.where(at, gcol_s[pl.ds(e, 1), :], 0.0), axis=1, keepdims=True)
                    drow = jnp.exp(cume - crow + bias_s[pl.ds(c * CH + e, 1), :])
                    f = amp * st_s[r, c] + dot_twin(kt_s[hk * NC + c] * drow, u_s[r, c])

                    @pl.when(opens)
                    def _():
                        b1_ref[h] = f[:, :D]
                        m1_ref[h] = f[:, D:]

                    @pl.when(jnp.logical_not(opens))
                    def _():
                        unit = lax.rem(hk, 2) * 8 + p * 2 + r
                        f0_ref[lax.rem(hk // 2, 2) * 4 + hk // 4, unit] = f[:, :D].T


def local_terms(lengths, q, k, v, ld, be):
    hm = jax.ShapeDtypeStruct((H, D, D), F32)
    tokens = jax.ShapeDtypeStruct((H, TOK, D), F32)
    vm = pltpu.VMEM
    return pl.pallas_call(
        terms_kernel,
        out_shape=(
            tokens, tokens, hm, hm, hm,
            jax.ShapeDtypeStruct((8, 16, D, D), F32),
            jax.ShapeDtypeStruct((8, D), F32),
        ),
        in_specs=[SMEM] + [VMEM] * 5,
        out_specs=tuple([VMEM] * 7),
        scratch_shapes=[
            vm((HK, TOK, D), F32),
            vm((HK, TOK, D), F32),
            vm((HK * NC, D, D), F32),
            vm((HK * NC * CH, D), F32),
            vm((HK * NC, CH, D), F32),
            vm((CH * CH, D), F32),
            vm((CH * CH, D), F32),
            vm((D * CH, D), F32),
            vm((D, D), F32),
            vm((D, D), F32),
            vm((CH, D), F32),
            vm((CH, D), F32),
            vm((CH, D), F32),
            vm((CH, D), jnp.int32),
            vm((TOK, D), F32),
            vm((CH, D), F32),
            vm((CH, D), F32),
            vm((2, NC, D, 2 * D), F32),
            vm((2, NC, CH, 2 * D), F32),
        ],
        compiler_params=pltpu.CompilerParams(vmem_limit_bytes=60 * 1024 * 1024),
        name="local_terms",
    )(lengths, q, k, v, ld, be)


def lines(me_ctx, me_grp):
    y, z = me_grp // 4, lax.rem(me_grp, 4)
    core = lax.rem(me_ctx, 2)

    def turn(i, by):
        return lax.rem(i + by, 4)

    return dict(
        twin={"ctx": me_ctx + 1 - 2 * core},
        chain={"ctx": lax.rem(me_ctx + 7 + 2 * core, 8)},
        x=({"ctx": lax.rem(me_ctx + 2, 8)}, {"ctx": lax.rem(me_ctx + 6, 8)}),
        z=({"grp": y * 4 + turn(z, 1)}, {"grp": y * 4 + turn(z, 3)}),
        y=({"grp": turn(y, 1) * 4 + z}, {"grp": turn(y, 3) * 4 + z}),
    )


class Copies:
    def __init__(self, send_sem, recv_sem):
        self.send_sem, self.recv_sem, self.made = send_sem, recv_sem, []

    def start(self, src, dst, device):
        i = len(self.made)
        made = pltpu.make_async_remote_copy(
            src_ref=src,
            dst_ref=dst,
            send_sem=self.send_sem.at[i],
            recv_sem=self.recv_sem.at[i],
            device_id=device,
            device_id_type=MESH,
        )
        made.start()
        self.made.append(made)
        return made

    def finish(self):
        for made in self.made:
            made.wait_send()


def add_units(dst, at, lo, n, src):
    @pl.loop(0, n)
    def _(u):
        dst[at, lo + u] = dst[at, lo + u] + src[u]


def sum_ring_begin(copies, buf, m, pos, pair, ra, rb, rc, rd):
    nxt, opp, prv = (lax.rem(pos + i, 4) for i in (1, 2, 3))
    up, down = pair
    c0 = copies.start(buf.at[opp, pl.ds(0, m)], ra, up)
    c1 = copies.start(buf.at[opp, pl.ds(m, m)], rb, down)
    c2 = copies.start(buf.at[nxt, pl.ds(m, m)], rc.at[pl.ds(m, m)], up)
    c3 = copies.start(buf.at[prv, pl.ds(0, m)], rd.at[pl.ds(0, m)], down)
    return c0, c1, c2, c3


def sum_ring_pass(copies, buf, m, pos, pair, ra, rb, rc, rd, begun):
    nxt, prv = lax.rem(pos + 1, 4), lax.rem(pos + 3, 4)
    up, down = pair
    c0, c1, c2, c3 = begun
    c0.wait_recv()
    add_units(buf, nxt, 0, m, ra)
    c4 = copies.start(buf.at[nxt, pl.ds(0, m)], rc.at[pl.ds(0, m)], up)
    c1.wait_recv()
    add_units(buf, prv, m, m, rb)
    c5 = copies.start(buf.at[prv, pl.ds(m, m)], rd.at[pl.ds(m, m)], down)
    return c2, c3, c4, c5


def chain_kernel(
    idx_ref, m_ref, b1_ref, bo_ref, flag_ref, f0_ref, in_ref, dec_ref,
    out_s, end_s, twin_s, xa, xb, xc, xd, got_a, got_b, put_s, ya, yb, yc, yd,
    chain_send, chain_recv, send_sem, recv_sem,
):
    me = lax.axis_index("ctx")
    grp = lax.axis_index("grp")
    core, chip = lax.rem(me, 2), me // 2
    at = lines(me, grp)
    barrier = pltpu.get_barrier_semaphore()
    for device in (at["twin"], at["chain"], *at["x"], *at["y"], *at["z"]):
        pl.semaphore_signal(barrier, inc=1, device_id=device, device_id_type=MESH)
    pl.semaphore_wait(barrier, 8)
    copies = Copies(send_sem, recv_sem)
    got_s = (got_a, got_b)

    def pass_on(h):
        return pltpu.make_async_remote_copy(
            src_ref=out_s.at[h],
            dst_ref=in_ref.at[h],
            send_sem=chain_send.at[h],
            recv_sem=chain_recv.at[h],
            device_id={"ctx": lax.rem(me + 1, 8)},
            device_id_type=MESH,
        )

    @pl.when(me == 0)
    def _():
        @pl.loop(0, H)
        def _(h):
            in_ref[h] = jnp.zeros((D, D), F32)

    twins = []
    for c in range(4):

        @pl.loop(0, 8)
        def _(j, c=c):
            h = c * 8 + j

            @pl.when(me > 0)
            def _():
                pass_on(h).wait_recv()

            x = dot_wide(m_ref[h], in_ref[h])
            out_s[h] = x * flag_ref[0:1, :] + bo_ref[h]

            @pl.when(me < 7)
            def _():
                pass_on(h).start()

            xt = (x + b1_ref[h]).T
            k, unit = j // 4, (lax.rem(j, 4) // 2) * 8 + lax.rem(j, 2)
            for p in range(REQS):
                here = flag_ref[1 + p : 2 + p, :]
                end_s[k * 4 + c, unit + 2 * p] = f0_ref[k * 4 + c, unit + 2 * p] + here * xt

        twins.append(copies.start(end_s.at[(1 - core) * 4 + c], twin_s.at[c], at["twin"]))

    for c in range(4):
        twins[c].wait_recv()

        @pl.loop(0, 16)
        def _(u, c=c):
            twin_s[c, u] = twin_s[c, u] + end_s[core * 4 + c, u]

    bufs = (xa, xb, xc, xd)
    begun = sum_ring_begin(copies, twin_s, 8, chip, at["x"], *bufs)
    rest = sum_ring_pass(copies, twin_s, 8, chip, at["x"], *bufs, begun)
    for made in rest:
        made.wait_recv()
    y, z = grp // 4, lax.rem(grp, 4)
    places = ((z, at["z"], y, at["y"]), (y, at["y"], z, at["z"]))

    for half, (pos, _pair, _, _) in enumerate(places):

        @pl.loop(0, 8)
        def _(u, half=half, pos=pos):
            i = half * 8 + u
            got_s[half][pos * 8 + u] = twin_s[chip, i] + xc[i] + xd[i]

    direct = []
    for half, (pos, pair, _, _) in enumerate(places):
        mine = got_s[half].at[pl.ds(pos * 8, 8)]
        direct.append((copies.start(mine, mine, pair[0]), copies.start(mine, mine, pair[1])))
    onward = []
    for half, (pos, pair, _, _) in enumerate(places):
        nxt, prv = lax.rem(pos + 1, 4), lax.rem(pos + 3, 4)
        direct[half][0].wait_recv()
        part = got_s[half].at[pl.ds(prv * 8, 4)]
        c0 = copies.start(part, part, pair[0])
        direct[half][1].wait_recv()
        part = got_s[half].at[pl.ds(nxt * 8 + 4, 4)]
        c1 = copies.start(part, part, pair[1])
        onward.append((c0, c1))
    begun = []
    for half, (_, _, pos, pair) in enumerate(places):
        onward[half][0].wait_recv()
        onward[half][1].wait_recv()

        @pl.loop(0, 16)
        def _(i, half=half):
            src = idx_ref[half, i]
            for h2 in range(2):
                x = got_s[half][jnp.maximum(src, 0) * 2 + h2]
                put_s[half * 4 + i // 4, lax.rem(i, 4) * 2 + h2] = jnp.where(src >= 0, x, 0.0)

        bufs = tuple(b.at[half] for b in (ya, yb, yc, yd))
        put = put_s.at[pl.ds(half * 4, 4)]
        begun.append(sum_ring_begin(copies, put, 4, pos, pair, *bufs))
    rest = []
    for half, (_, _, pos, pair) in enumerate(places):
        bufs = tuple(b.at[half] for b in (ya, yb, yc, yd))
        put = put_s.at[pl.ds(half * 4, 4)]
        rest.append(sum_ring_pass(copies, put, 4, pos, pair, *bufs, begun[half]))
    for half, (_, _, pos, pair) in enumerate(places):
        for made in rest[half]:
            made.wait_recv()

        @pl.loop(0, 8)
        def _(u, half=half, pos=pos):
            x = put_s[half * 4 + pos, u] + yc[half, u] + yd[half, u]
            dec_ref[u // 2, half * 2 + lax.rem(u, 2)] = x

    @pl.when(me < 7)
    def _():
        @pl.loop(0, H)
        def _(h):
            pass_on(h).wait_send()

    copies.finish()


def chain(idx, m1, b1, bo, flag, f0):
    vm = pltpu.VMEM

    def units(*n):
        return vm(n + (D, D), F32)

    return pl.pallas_call(
        chain_kernel,
        out_shape=(
            jax.ShapeDtypeStruct((H, D, D), F32),
            jax.ShapeDtypeStruct((REQS, REQS, D, D), F32),
        ),
        in_specs=[SMEM] + [VMEM] * 5,
        out_specs=(VMEM, VMEM),
        scratch_shapes=[
            units(H), units(8, 16), units(4, 16),
            units(8), units(8), units(16), units(16),
            units(32), units(32), units(8, 8),
            units(2, 4), units(2, 4), units(2, 8), units(2, 8),
            pltpu.SemaphoreType.DMA((H,)),
            pltpu.SemaphoreType.DMA((H,)),
            pltpu.SemaphoreType.DMA((32,)),
            pltpu.SemaphoreType.DMA((32,)),
        ],
        compiler_params=pltpu.CompilerParams(
            collective_id=0, has_side_effects=True, vmem_limit_bytes=60 * 1024 * 1024
        ),
        name="state_chain",
    )(idx, m1, b1, bo, flag, f0)


HB = 8


def gate_kernel(out0_ref, qe_ref, x_ref, gate_ref, gain_ref, o_ref):
    gain = gain_ref[...]
    gate = gate_ref.reshape(TOK * HB, D)
    dst = o_ref.reshape(TOK * HB, D)
    for h in range(HB):
        raw = out0_ref[h] + dot_wide(qe_ref[h], x_ref[h])
        ms = jnp.sum(raw * raw, axis=1, keepdims=True) * (1.0 / D)
        g = gate[pl.ds(h, TOK, stride=HB), :]
        act = g / (1.0 + jnp.exp(-g))
        dst[pl.ds(h, TOK, stride=HB), :] = raw * lax.rsqrt(ms + 1e-6) * gain * act


def gated_out(out0, qe, x_in, gate, gain):
    tok = pl.BlockSpec((HB, TOK, D), lambda i: (i, 0, 0))
    nat = pl.BlockSpec((TOK, HB, D), lambda i: (0, i, 0))
    return pl.pallas_call(
        gate_kernel,
        grid=(H // HB,),
        out_shape=jax.ShapeDtypeStruct((TOK, H, D), F32),
        in_specs=[
            tok, tok,
            pl.BlockSpec((HB, D, D), lambda i: (i, 0, 0)),
            nat,
            pl.BlockSpec((1, D), lambda i: (0, 0)),
        ],
        out_specs=nat,
        compiler_params=pltpu.CompilerParams(vmem_limit_bytes=40 * 1024 * 1024),
        cost_estimate=pl.CostEstimate(flops=800000000, bytes_accessed=20000000, transcendentals=0),
        name="gated_out",
    )(out0, qe, x_in, gate, gain)


def routes(owner_slot):
    me = lax.axis_index("grp")
    y, z = me // 4, me % 4
    other = jnp.arange(4)
    along_z, along_y = y * 4 + other, other * 4 + z
    out = []
    for sources, targets in ((along_z, along_y), (along_y, along_z)):
        slots = owner_slot.reshape(16, REQS)[sources].reshape(-1)
        wanted = (targets[:, None] * REQS + jnp.arange(REQS)[None, :]).reshape(-1)
        hit = wanted[:, None] == slots[None, :]
        out.append(jnp.max(jnp.where(hit, jnp.arange(16)[None, :], -1), axis=1))
    return jnp.stack(out).astype(jnp.int32)


def local(
    queries, key_vecs, val_vecs, out_gate, log_decay, beta_gate, norm_gain, lengths, owner_slot
):
    def rows(x):
        x = x[0].reshape(HK, 2, NC, CH).transpose(1, 0, 2, 3).reshape(D, CH)
        return jnp.concatenate([x, x], axis=1)

    out0, qe, m1, b1, bo, f0, flag = local_terms(
        lengths,
        queries.reshape(TOK * HK, D),
        key_vecs.reshape(TOK * HK, D),
        val_vecs.reshape(TOK * H, D),
        rows(log_decay),
        rows(beta_gate),
    )
    x_in, decode = chain(routes(owner_slot), m1, b1, bo, flag, f0)
    attn = gated_out(out0, qe, x_in, out_gate[0], norm_gain.reshape(1, D))
    return attn[None], decode


def solution(mesh):
    return jax.shard_map(
        local,
        mesh=mesh,
        in_specs=(
            P("grp", "ctx", None, None),
            P("grp", "ctx", None, None),
            P("grp", "ctx", None, None),
            P("grp", "ctx", None, None),
            P("grp", None, "ctx"),
            P("grp", None, "ctx"),
            P(),
            P("grp", None),
            P(),
        ),
        out_specs=(P("grp", "ctx", None, None), P("grp", "ctx", None, None)),
        check_vma=False,
    )
```

time: 1300 us -> 248 us (0.19)
  local copies, waits for them, and re-layouts: 351 us -> 10.9 us
  waiting for transfers between devices: 312 us -> 0 us
  other arithmetic: 305 us -> 1.86 us
  matrix products: 273 us -> 0 us
  Pallas kernels: 0 us -> 230 us
  starting transfers between devices: 29.1 us -> 0 us
  between operations: 14.7 us -> 0.74 us
    another operation x9 -> x1, other arithmetic: 267 us -> 0.56 us  [routes(): return jnp.stack(out).astype(jnp.int32)]
    dot_general x38 -> x0, matrix products: 262 us -> none  [the longest x21 103 us: batch_mm(): jnp.einsum('...ij,...jk->...ik', left_mat, right_mat, precision=exact_mode)]
    dynamic_update_slice x8 -> x0, local copies, waits for them, and re-layouts: 236 us -> none  [run_blocks(): lax.scan(advance, incoming, (out_base, query_eff, write_keys, upd_base, t...]
    pallas_call x0 -> x3, Pallas kernels: none -> 230 us  [the longest x1 150 us: chain(): pl.pallas_call(chain_kernel, out_shape=(jax.ShapeDtypeStruct((H, D, D), F...]
    ppermute x7 -> x0, waiting for transfers between devices: 163 us -> none  [shifted(): return lax.ppermute(block, axis, route)]
    all_gather x1 -> x0, waiting for transfers between devices: 94.7 us -> none  [local(): lax.all_gather(own_states, 'grp', axis=0, tiled=True)]
    reduce_scatter x1 -> x0, waiting for transfers between devices: 54.6 us -> none  [local(): lax.psum_scatter(end_buf, 'ctx', scatter_dimension=1, tiled=True)]
    mul x5 -> x2, other arithmetic: 29.4 us -> 0.01 us  [routes(): wanted = (targets[:, None] * REQS + jnp.arange(REQS)[None, :]).reshape(-1)]
  transfers between devices with their start and end apart: 9 -> 0, of which waited for: 9 -> 0; matrix products, arithmetic and copies ran while one was open for 1% -> 0% of each run, Pallas kernels for 0% -> 0%
where the time goes in v1:
time: 248 us; the launch traced here: 244 us
  Pallas kernels  230 us (93%)
  local copies, waits for them, and re-layouts  10.9 us (4%)
    pallas_call x1, Pallas kernels, chain(): pl.pallas_call(chain_kernel, out_shape=(jax.ShapeDtypeStruct((H, D, D), F...  150 us
    pallas_call x1, Pallas kernels, local_terms(): pl.pallas_call(terms_kernel, out_shape=(tokens, tokens, hm, hm, hm, jax.S...  73 us
    unnamed x11, local copies, waits for them, and re-layouts  6.94 us
    pallas_call x1, Pallas kernels, gated_out(): pl.pallas_call(gate_kernel, grid=(H // HB,), out_shape=jax.ShapeDtypeStru...  6.92 us

profile of v1, /device:TPU:5, one launch (start us, length us, event | category | flops | bytes accessed | tf_op | source)
XLA Modules:
  0.0 243.8 jit_solution(18295094631141369700)
XLA Ops:
  0.7 0.1 iota_add_fusion.1
  0.8 0.1 add.111
  0.9 0.1 iota_add_fusion
  0.9 0.1 add.120
  1.0 0.7 reshape.104
  1.8 0.6 gather_fusion.1
  2.3 0.6 gather_fusion
  2.9 0.1 eq.33
  3.0 0.1 eq.37
  3.1 0.2 select_reduce_fusion
  3.3 0.2 select_reduce_fusion.1
  3.4 0.6 pad_add_fusion.idx_ref
  4.0 0.8 reshape_squeeze.6
  4.9 0.8 reshape_squeeze.7
  5.7 0.8 pad_maximum_fusion
  6.5 73.0 %local_terms.1 = (f32[32,256,128]{2,1,0:T(8,128)}, f32[32,256,128]{2,1,0:T(8,128)}, f32[32,128,128]{2,1,0:T(8,128)}, f32[32,128,128]{2,1,0:T(8,128)}, f32[32,128...) custom-call(s32[1,4]{1,0:T(1,128)} %len_ref.1, f32[4096,128]{1,0:T(8,128)} %bitcast.22, ...), custom_call_target="tpu_custom_call" | custom-call | tf_op jit(solution)/shard_map/local_terms/pallas_call | solution.py:246
  79.5 0.0 copy-start.3
  79.5 150.3 %state_chain.1 = (f32[32,128,128]{2,1,0:T(8,128)}, f32[4,4,128,128]{3,2,1,0:T(8,128)}) custom-call(s32[2,16]{1,0:T(2,128)} %pad_add_fusion.idx_ref, f32[32,128,128]{2,1,0:T(8,128)} %get-tuple-element.13.m_ref, f32[32,128,128]{2,1,0:T(8,128)} %get-tuple-element.14.b1_ref, f32[32,128,128]{2,1,0:T(8,128)} %get-tuple-element.15.bo_ref, ...), custom_call_target="tpu_custom_call" | custom-call | tf_op jit(solution)/shard_map/state_chain/pallas_call | solution.py:487
  229.9 0.0 copy-done.3
  229.9 0.0 copy-start
  229.9 2.2 copy-done
  232.1 0.0 copy-start.1
  232.1 2.2 copy-done.1
  234.3 0.0 copy-start.2
  234.3 1.6 copy-done.2
  235.9 0.0 copy-start.4
  235.9 6.9 %gated_out.1 = f32[256,32,128]{2,1,0:T(8,128)} custom-call(f32[32,256,128]{2,1,0:T(8,128)S(1)} %copy-done, f32[32,256,128]{2,1,0:T(8,128)S(1)} %copy-done.1, f32[32,128,128]{2,1,0:T(8,128)S(1)} %copy-done.2, f32[256,32,128]{2,1,0:T(8,128)} %bitcast.20, f32[1,128]{1,0:T(1,128)S(1)} %bitcast.18), custom_call_target="tpu_custom_call" | custom-call | flops 800000000 | bytes 20000000 | tf_op jit(solution)/shard_map/gated_out/pallas_call | solution.py:530
  242.8 0.0 copy-done.4
  242.8 1.0 copy.18
  (8 shorter events, 0.1 us)
Async XLA Ops:
  79.5 150.4 %copy-start.3 = (f32[128]{0:T(128)S(1)}, f32[128]{0:T(128)}, u32[]{:S(2)}) copy-start(f32[128]{0:T(128)} %param.15) | copy-start | bytes 1540
  229.9 2.2 copy-start
  232.1 2.2 copy-start.1
  234.3 1.6 copy-start.2
  235.9 6.9 %copy-start.4 = (f32[4,4,128,128]{3,2,1,0:T(8,128)S(1)}, f32[4,4,128,128]{3,2,1,0:T(8,128)}, u32[]{:S(2)}) copy-start(f32[4,4,128,128]{3,2,1,0:T(8,128)} %get-tuple-element.25) | copy-start | bytes 3145732

commit v2 on v1

v2 whole, which is shorter than its diff:
```python
import jax
import jax.numpy as jnp
from jax import lax
from jax.experimental import pallas as pl
from jax.experimental.pallas import tpu as pltpu
from jax.sharding import PartitionSpec as P

CH = 64
D = 128
HK = 16
H = 32
TOK = 256
NC = TOK // CH
REQS = 4
NI = 2
F32 = jnp.float32
BF16 = jnp.bfloat16
MESH = pl.DeviceIdType.MESH
VMEM = pl.BlockSpec(memory_space=pltpu.VMEM)
SMEM = pl.BlockSpec(memory_space=pltpu.SMEM)
ANY = pl.BlockSpec(memory_space=pl.ANY)


def mm(x, y):
    return lax.dot_general(x, y, (((1,), (0,)), ((), ())), preferred_element_type=F32)


def split(x):
    hi = x.astype(BF16)
    return hi, (x - hi.astype(F32)).astype(BF16)


def dot_wide(x, y):
    xh, xl = split(x)
    yh, yl = split(y)
    left = jnp.concatenate([xh, xl], axis=1)
    return mm(left, jnp.concatenate([yh, yh], axis=0)) + mm(xh, yl)


def dot_twin(x, y):
    low = x - x.astype(BF16).astype(F32)
    lane = lax.broadcasted_iota(jnp.int32, x.shape, 1)
    s = jnp.where(lane < CH, x, low).astype(BF16)
    yh, yl = split(y)
    left = jnp.concatenate([s, s], axis=1)
    return mm(left, jnp.concatenate([yh, yh, yl, yl], axis=0))


def prompt_ends(len_ref):
    ends = [len_ref[0, 0]]
    for r in range(1, REQS):
        ends.append(ends[-1] + len_ref[0, r])
    return ends


def seg_start(pos, ends):
    start = jnp.zeros(pos.shape, jnp.int32)
    for e in ends[:-1]:
        start = jnp.where(pos >= e, e, start)
    return start


def terms_kernel(
    len_ref, q_ref, k_ref, v_hbm, ld_ref, be_ref,
    out0_hbm, qe_hbm, m1_hbm, b1_hbm, bo_hbm, f0_hbm, flag_ref,
    out0_ref, qe_ref, m1_ref, b1_ref, bo_ref, f0_ref, v_ref, out_sem, in_sem,
    kn_s, qn_s, kt_s, gram_s, qk_s, low_s, inv_s, t_s,
    cum_s, gam_s, cumt_s, gamt_s, bet_s, start_s, bias_s, col_s, gcol_s, st_s, u_s,
):
    load_v = pltpu.make_async_copy(v_hbm, v_ref, in_sem.at[0])
    load_v.start()
    off = lax.axis_index("ctx") * TOK
    ends = prompt_ends(len_ref)
    lane = lax.broadcasted_iota(jnp.int32, (D, D), 1)
    row = lax.broadcasted_iota(jnp.int32, (D, D), 0)

    tok = lane % CH
    for i, src in enumerate((ld_ref, be_ref)):
        x = src[...]
        low_s[2 * i * H : (2 * i + 1) * H, :] = x[:, :D]
        low_s[(2 * i + 1) * H : (2 * i + 2) * H, :] = x[:, D:]
    for c in range(NC):
        for r in range(2):
            for i, dst in enumerate((cum_s, gam_s)):
                x = low_s[pl.ds((2 * i + c // 2) * H + r, HK, stride=2), :]
                y = pltpu.roll(x, CH, 1)
                x = jnp.where((lane[:HK] < CH) == (c % 2 == 0), x, y)
                dst[pl.ds(r * CH + c, HK, stride=NC), :] = x
    cum = cum_s[...]
    beta = gam_s[...]
    for s in (1, 2, 4, 8, 16, 32):
        cum = cum + jnp.where(tok >= s, pltpu.roll(cum, s, 1), 0.0)
    lo_a = off + (row % NC) * CH
    carry_a = seg_start(lo_a + tok, ends) < lo_a
    gam = jnp.where(carry_a, jnp.exp(cum), 0.0)
    cum_s[...] = cum
    gam_s[...] = gam
    cumt_s[...] = cum.T[:CH]
    gamt_s[...] = gam.T[:CH]
    bet_s[...] = beta.T[:CH]
    lane_b = lane[:CH]
    row_b = row[:CH]
    start_s[...] = seg_start(off + (lane_b % NC) * CH + row_b, ends)
    tok_b = tok[:CH]
    for c in range(NC):
        lo = off + c * CH
        same = seg_start(lo + row_b, ends) == seg_start(lo + tok_b, ends)
        bias_s[pl.ds(c * CH, CH), :] = jnp.where(same & (tok_b <= row_b), 0.0, -1e30)

    @pl.loop(0, 8)
    def _(i):
        for u in range(16):
            f0_ref[i, u // 4, u % 4] = jnp.zeros((D, D), F32)

    @pl.loop(0, HK, unroll=4)
    def _(hk):
        k = k_ref[pl.ds(hk, TOK, stride=HK), :]
        q = q_ref[pl.ds(hk, TOK, stride=HK), :]
        kn = k * lax.rsqrt(jnp.sum(k * k, axis=1, keepdims=True) + 1e-6)
        qn = q * (lax.rsqrt(jnp.sum(q * q, axis=1, keepdims=True) + 1e-6) * (D**-0.5))
        kn_s[hk] = kn
        qn_s[hk] = qn
        for c in range(NC):
            kc = kn[c * CH : (c + 1) * CH]
            qc = qn[c * CH : (c + 1) * CH]
            kt = jnp.concatenate([kc, kc], axis=0).T
            kt_s[hk * NC + c] = kt
            g = dot_wide(jnp.concatenate([kc, qc], axis=0), kt)
            gram_s[pl.ds((hk * NC + c) * CH, CH), :] = g[:CH]
            qk_s[hk * NC + c] = g[CH:]

    @pl.loop(0, CH, unroll=8)
    def _(i):
        x = gram_s[pl.ds(i, HK * NC, stride=CH), :]
        xt = jnp.concatenate([x, x], axis=0).T[:CH]
        keep = (start_s[...] == start_s[pl.ds(i, 1), :]) & (row_b < i)
        decay = jnp.exp(jnp.where(keep, cumt_s[pl.ds(i, 1), :] - cumt_s[...], -1e30))
        low_s[pl.ds(i * CH, CH), :] = xt * decay * bet_s[pl.ds(i, 1), :]

    for g in range(CH // 4):
        n = 8 * ((4 * g + 3) // 8 + 1)
        rid = lax.broadcasted_iota(jnp.int32, (n, D), 0)
        acc = tuple(jnp.where(rid == 4 * g + a, 1.0, 0.0).astype(F32) for a in range(4))

        def body(jb, acc, g=g, n=n):
            acc = list(acc)
            for b in range(4):
                t = inv_s[pl.ds((jb * 4 + b) * CH, n), :]
                for a in range(4):
                    acc[a] = acc[a] - low_s[pl.ds((4 * g + a) * CH + jb * 4 + b, 1), :] * t
            return tuple(acc)

        if g:
            acc = lax.fori_loop(0, g, body, acc)
        acc = list(acc)
        for a in range(4):
            for b in range(a):
                acc[a] = acc[a] - low_s[pl.ds((4 * g + a) * CH + 4 * g + b, 1), :] * acc[b]
            inv_s[pl.ds((4 * g + a) * CH, n), :] = acc[a]
            if n < CH:
                inv_s[pl.ds((4 * g + a) * CH + n, CH - n), :] = jnp.zeros((CH - n, D), F32)

    @pl.loop(0, CH, unroll=8)
    def _(i):
        x = inv_s[pl.ds(i * CH, CH), :] * bet_s[...]
        t_s[pl.ds(i, D, stride=CH), :] = jnp.concatenate([x, x], axis=0).T

    first_end = ends[-1]
    for e in ends[-2::-1]:
        first_end = jnp.where(e > off, e, first_end)
    marks = [first_end >= off + TOK]
    begin = 0
    for e in ends:
        marks.append((begin <= off) & (e > off) & (e <= off + TOK))
        begin = e
    mark = jnp.zeros((8, D), F32)
    for i, m in enumerate(marks):
        mark = jnp.where(row[:8] == i, jnp.where(m, 1.0, 0.0), mark)
    flag_ref[...] = mark

    eye = jnp.where(lane == row, 1.0, 0.0).astype(F32)
    zero = jnp.zeros((CH, D), F32)

    pairs = [(i, r) for i in range(NI) for r in range(2)]
    load_v.wait()

    def store(step):
        made = []
        at = pl.ds(step * 2 * NI, 2 * NI)
        for i, (a, b) in enumerate(((out0_ref, out0_hbm), (qe_ref, qe_hbm))):
            made.append(pltpu.make_async_copy(a.at[at], b.at[at], out_sem.at[step, i]))
        for j in range(4):
            for i, (a, b) in enumerate(((m1_ref, m1_hbm), (b1_ref, b1_hbm), (bo_ref, bo_hbm))):
                at = j * 8 + step
                made.append(pltpu.make_async_copy(a.at[at], b.at[at], out_sem.at[step, 2 + 3 * j + i]))
        return made

    @pl.loop(0, HK // NI)
    def _(step):
        hks = [step * NI + i for i in range(NI)]
        shift = lax.rem(D - step * (NI * NC), D)
        col_s[...] = pltpu.roll(cumt_s[...], shift, 1)
        gcol_s[...] = pltpu.roll(gamt_s[...], shift, 1)
        col = col_s[...]
        gcol = gcol_s[...]
        state = {}
        for c in range(NC):
            bias = bias_s[pl.ds(c * CH, CH), :]
            for i, r in pairs:
                hk = hks[i]
                h = hk * 2 + r
                kc = kn_s[hk, pl.ds(c * CH, CH), :]
                qc = qn_s[hk, pl.ds(c * CH, CH), :]
                kt = kt_s[hk * NC + c]
                qk = qk_s[hk * NC + c]
                at = r * CH + i * NC + c
                b = r * CH + hk * NC + c
                ccol = col[:, at : at + 1]
                gc = gcol[:, at : at + 1]
                decay = jnp.exp(ccol - cum_s[pl.ds(b, 1), :] + bias)
                v = v_ref[pl.ds(c * CH * H + h, CH, stride=H), :]
                gq = qc * gc
                uw = dot_twin(t_s[pl.ds(b * CH, CH), :], jnp.concatenate([v, kc * gc], axis=1))
                u0, w = uw[:, :D], uw[:, D:]
                if c == 0:
                    old = jnp.concatenate([jnp.zeros((D, D), F32), eye], axis=1)
                    u = jnp.concatenate([u0, -w], axis=1)
                    base = jnp.concatenate([zero, gq], axis=1)
                else:
                    old = state[i, r]
                    p = dot_wide(jnp.concatenate([w, gq], axis=0), old)
                    u = jnp.concatenate([u0, zero], axis=1) - p[:CH]
                    base = p[CH:]
                left = jnp.concatenate([qk * decay, kt * decay[CH - 1 : CH]], axis=0)
                res = dot_twin(left, u)
                o = base + res[:CH]
                out0_ref[h, pl.ds(c * CH, CH), :] = o[:, :D]
                qe_ref[h, pl.ds(c * CH, CH), :] = o[:, D:]
                st_s[i, r, c] = old
                u_s[i, r, c] = u
                state[i, r] = gc[CH - 1 : CH] * old + res[CH:]
        for i, r in pairs:
            h = hks[i] * 2 + r
            bo_ref[i * 16 + r * 8 + step] = state[i, r][:, :D]
            b1_ref[i * 16 + r * 8 + step] = state[i, r][:, :D]
            m1_ref[i * 16 + r * 8 + step] = state[i, r][:, D:]
        begin = 0
        for p in range(REQS):
            last = ends[p] - 1 - off
            here = (last >= 0) & (last < TOK)
            opens = begin <= off
            begin = ends[p]
            c = last // CH
            e = last % CH

            def scaled(i, r, c=c, e=e):
                at = lane[:1] == r * CH + i * NC + c
                crow = cum_s[pl.ds(r * CH + hks[i] * NC + c, 1), :]
                cume = jnp.sum(jnp.where(at, col_s[pl.ds(e, 1), :], 0.0), axis=1, keepdims=True)
                amp = jnp.sum(jnp.where(at, gcol_s[pl.ds(e, 1), :], 0.0), axis=1, keepdims=True)
                drow = jnp.exp(cume - crow + bias_s[pl.ds(c * CH + e, 1), :])
                return amp, kt_s[hks[i] * NC + c] * drow

            @pl.when(here & opens)
            def _(c=c, scaled=scaled):
                for i, r in pairs:
                    amp, kd = scaled(i, r)
                    f = amp * st_s[i, r, c] + dot_twin(kd, u_s[i, r, c])
                    b1_ref[i * 16 + r * 8 + step] = f[:, :D]
                    m1_ref[i * 16 + r * 8 + step] = f[:, D:]

            @pl.when(here & jnp.logical_not(opens))
            def _(c=c, p=p, scaled=scaled):
                for i, r in pairs:
                    amp, kd = scaled(i, r)
                    f = amp * st_s[i, r, c, :, :D] + dot_twin(kd, u_s[i, r, c, :, :D])
                    h = hks[i] * 2 + r
                    f0_ref[lax.rem(h, 4) * 2 + lax.rem(h // 4, 2), h // 8, p] = f.T

        for made in store(step):
            made.start()

    store_f0 = pltpu.make_async_copy(f0_ref, f0_hbm, in_sem.at[1])
    store_f0.start()

    @pl.loop(0, HK // NI)
    def _(step):
        for made in store(step):
            made.wait()

    store_f0.wait()


def local_terms(lengths, q, k, v, ld, be):
    hm = jax.ShapeDtypeStruct((H, D, D), F32)
    tokens = jax.ShapeDtypeStruct((H, TOK, D), F32)
    vm = pltpu.VMEM
    return pl.pallas_call(
        terms_kernel,
        out_shape=(
            tokens, tokens, hm, hm, hm,
            jax.ShapeDtypeStruct((8, 4, REQS, D, D), F32),
            jax.ShapeDtypeStruct((8, D), F32),
        ),
        in_specs=[SMEM, VMEM, VMEM, ANY, VMEM, VMEM],
        out_specs=tuple([ANY] * 6 + [VMEM]),
        scratch_shapes=[
            vm((H, TOK, D), F32),
            vm((H, TOK, D), F32),
            vm((H, D, D), F32),
            vm((H, D, D), F32),
            vm((H, D, D), F32),
            vm((8, 4, REQS, D, D), F32),
            vm((TOK * H, D), F32),
            pltpu.SemaphoreType.DMA((HK // NI, 14)),
            pltpu.SemaphoreType.DMA((2,)),
            vm((HK, TOK, D), F32),
            vm((HK, TOK, D), F32),
            vm((HK * NC, D, D), F32),
            vm((HK * NC * CH, D), F32),
            vm((HK * NC, CH, D), F32),
            vm((CH * CH, D), F32),
            vm((CH * CH, D), F32),
            vm((D * CH, D), F32),
            vm((D, D), F32),
            vm((D, D), F32),
            vm((CH, D), F32),
            vm((CH, D), F32),
            vm((CH, D), F32),
            vm((CH, D), jnp.int32),
            vm((TOK, D), F32),
            vm((CH, D), F32),
            vm((CH, D), F32),
            vm((NI, 2, NC, D, 2 * D), F32),
            vm((NI, 2, NC, CH, 2 * D), F32),
        ],
        compiler_params=pltpu.CompilerParams(vmem_limit_bytes=60 * 1024 * 1024),
        name="local_terms",
    )(lengths, q, k, v, ld, be)


def lines(me_ctx, me_grp):
    y, z = me_grp // 4, lax.rem(me_grp, 4)
    core = lax.rem(me_ctx, 2)

    def turn(i, by):
        return lax.rem(i + by, 4)

    return dict(
        twin={"ctx": me_ctx + 1 - 2 * core},
        chain={"ctx": lax.rem(me_ctx + 7 + 2 * core, 8)},
        x=({"ctx": lax.rem(me_ctx + 2, 8)}, {"ctx": lax.rem(me_ctx + 6, 8)}),
        z=({"grp": y * 4 + turn(z, 1)}, {"grp": y * 4 + turn(z, 3)}),
        y=({"grp": turn(y, 1) * 4 + z}, {"grp": turn(y, 3) * 4 + z}),
    )


class Copies:
    def __init__(self, send_sem, recv_sem):
        self.send_sem, self.recv_sem, self.made = send_sem, recv_sem, []

    def start(self, src, dst, device):
        i = len(self.made)
        made = pltpu.make_async_remote_copy(
            src_ref=src,
            dst_ref=dst,
            send_sem=self.send_sem.at[i],
            recv_sem=self.recv_sem.at[i],
            device_id=device,
            device_id_type=MESH,
        )
        made.start()
        self.made.append(made)
        return made

    def finish(self):
        for made in self.made:
            made.wait_send()


def add_units(dst, at, lo, n, src):
    for u in range(n):
        dst[at, lo + u] = dst[at, lo + u] + src[u]


def ring_ids(pos):
    return tuple(lax.rem(pos + i, 4) for i in (1, 2, 3))


def chain_kernel(
    own_ref, m_hbm, b1_hbm, bo_hbm, flag_ref, f0_hbm, in_ref, dec_ref,
    idx_ref, m_ref, b1_ref, bo_ref, load_sem, out_s, end_s, twin_s, xb, xc, xd, got_0, got_1, got_2, got_3, put_s, ya, yb, yc, yd,
    chain_send, chain_recv, send_sem, recv_sem,
):
    me = lax.axis_index("ctx")
    grp = lax.axis_index("grp")
    core, chip = lax.rem(me, 2), me // 2
    at = lines(me, grp)
    loads = []
    for j in range(4):
        rounds = [(a.at[pl.ds(8 * j, 8)], b.at[pl.ds(8 * j, 8)]) for a, b in
                  ((m_hbm, m_ref), (b1_hbm, b1_ref), (bo_hbm, bo_ref))]
        rounds.append((f0_hbm.at[pl.ds(2 * j, 2)], end_s.at[pl.ds(2 * j, 2)]))
        for i, (a, b) in enumerate(rounds):
            made = pltpu.make_async_copy(a, b, load_sem.at[4 * j + i])
            made.start()
            loads.append(made)

    y, z = grp // 4, lax.rem(grp, 4)
    for order in range(2):

        @pl.loop(0, 4)
        def _(t, order=order):
            line = (t * 4 + z) if order == 0 else (y * 4 + t)
            for slot in range(REQS):
                found = jnp.int32(-1)
                for i in range(16):
                    source = (y * 4 + i // 4) if order == 0 else ((i // 4) * 4 + z)
                    hit = own_ref[source * REQS + i % 4] == line * REQS + slot
                    found = jnp.where(hit, jnp.int32(i), found)
                idx_ref[order, t * REQS + slot] = found

    barrier = pltpu.get_barrier_semaphore()
    for device in (at["twin"], at["chain"], *at["x"], *at["y"], *at["z"]):
        pl.semaphore_signal(barrier, inc=1, device_id=device, device_id_type=MESH)
    pl.semaphore_wait(barrier, 8)
    copies = Copies(send_sem, recv_sem)
    got_s = (got_0, got_1, got_2, got_3)
    x_next, x_opp, x_prev = ring_ids(chip)
    x_up, x_down = at["x"]

    def pass_on(h):
        return pltpu.make_async_remote_copy(
            src_ref=out_s.at[h],
            dst_ref=in_ref.at[h],
            send_sem=chain_send.at[h],
            recv_sem=chain_recv.at[h],
            device_id={"ctx": lax.rem(me + 1, 8)},
            device_id_type=MESH,
        )

    @pl.when(me == 0)
    def _():
        @pl.loop(0, H)
        def _(h):
            in_ref[h] = jnp.zeros((D, D), F32)

    def advance(j):
        for made in loads[4 * j : 4 * j + 4]:
            made.wait()

        @pl.loop(0, 8)
        def _(e):
            h = e * 4 + j

            @pl.when(me > 0)
            def _():
                pass_on(h).wait_recv()

            x = dot_wide(m_ref[j * 8 + e], in_ref[h])
            out_s[h] = x * flag_ref[0:1, :] + bo_ref[j * 8 + e]

            @pl.when(me < 7)
            def _():
                pass_on(h).start()

            xt = (x + b1_ref[j * 8 + e]).T
            at, c = j * 2 + lax.rem(e, 2), e // 2
            for p in range(REQS):
                here = flag_ref[1 + p : 2 + p, :]
                end_s[at, c, p] = end_s[at, c, p] + here * xt

    twins, back, ahead, last = [], [], [], []

    def join(j):
        twins[j].wait_recv()

        @pl.loop(0, 4)
        def _(c):
            add_units(twin_s.at[j], c, 0, 4, end_s.at[j * 2 + core, c])

        back.append(copies.start(twin_s.at[j, x_opp], xb.at[j], x_down))

    def relay(j):
        back[j].wait_recv()
        add_units(twin_s.at[j], x_prev, 0, 4, xb.at[j])
        last.append(copies.start(twin_s.at[j, x_prev], xd.at[j], x_down))

    for j in range(4):
        advance(j)
        mine = end_s.at[j * 2 + 1 - core]
        twins.append(copies.start(mine, twin_s.at[j], at["twin"]))
        if j >= 1:
            join(j - 1)
    relay(0)
    ahead.append(copies.start(twin_s.at[0, x_next], xc.at[0], x_up))
    ahead.append(copies.start(twin_s.at[1, x_next], xc.at[1], x_up))
    join(3)
    relay(1)
    ahead.append(copies.start(twin_s.at[2, x_next], xc.at[2], x_up))
    ahead.append(copies.start(twin_s.at[3, x_next], xc.at[3], x_up))

    places = ((z, at["z"], y, at["y"]), (y, at["y"], z, at["z"]))
    direct, onward, begun, passed = [], [], [], []

    def spread(j):
        pos, (up, down), _, _ = places[j % 2]
        ahead[j].wait_recv()
        last[j].wait_recv()
        for u in range(4):
            got_s[j][pos * 4 + u] = twin_s[j, chip, u] + xc[j, u] + xd[j, u]
        mine = got_s[j].at[pl.ds(pos * 4, 4)]
        direct.append((copies.start(mine, mine, up), copies.start(mine, mine, down)))

    def forward(j):
        pos, (up, down), _, _ = places[j % 2]
        nxt, _, prv = ring_ids(pos)
        direct[j][0].wait_recv()
        part = got_s[j].at[pl.ds(prv * 4, 2)]
        c0 = copies.start(part, part, up)
        direct[j][1].wait_recv()
        part = got_s[j].at[pl.ds(nxt * 4 + 2, 2)]
        onward.append((c0, copies.start(part, part, down)))

    def pick(j):
        _, _, pos, (up, down) = places[j % 2]
        nxt, opp, prv = ring_ids(pos)
        onward[j][0].wait_recv()
        onward[j][1].wait_recv()

        @pl.loop(0, 4)
        def _(t):
            for s in range(REQS):
                src = idx_ref[j % 2, t * REQS + s]
                x = got_s[j][jnp.maximum(src, 0)]
                put_s[j * 4 + t, s] = jnp.where(src >= 0, x, 0.0)

        put = put_s.at[pl.ds(j * 4, 4)]
        c0 = copies.start(put.at[opp, pl.ds(0, 2)], ya.at[j], up)
        c1 = copies.start(put.at[opp, pl.ds(2, 2)], yb.at[j], down)
        c2 = copies.start(put.at[nxt, pl.ds(2, 2)], yc.at[j, pl.ds(2, 2)], up)
        c3 = copies.start(put.at[prv, pl.ds(0, 2)], yd.at[j, pl.ds(0, 2)], down)
        begun.append((c0, c1, c2, c3))

    def total(j):
        _, _, pos, (up, down) = places[j % 2]
        nxt, _, prv = ring_ids(pos)
        c0, c1, c2, c3 = begun[j]
        put = put_s.at[pl.ds(j * 4, 4)]
        c0.wait_recv()
        add_units(put, nxt, 0, 2, ya.at[j])
        c4 = copies.start(put.at[nxt, pl.ds(0, 2)], yc.at[j, pl.ds(0, 2)], up)
        c1.wait_recv()
        add_units(put, prv, 2, 2, yb.at[j])
        c5 = copies.start(put.at[prv, pl.ds(2, 2)], yd.at[j, pl.ds(2, 2)], down)
        passed.append((c2, c3, c4, c5))

    def settle(j):
        _, _, pos, _ = places[j % 2]
        for made in passed[j]:
            made.wait_recv()
        for s in range(REQS):
            dec_ref[s, j] = put_s[j * 4 + pos, s] + yc[j, s] + yd[j, s]

    spread(0)
    relay(2)
    spread(1)
    relay(3)
    forward(0)
    forward(1)
    spread(2)
    spread(3)
    pick(0)
    pick(1)
    forward(2)
    forward(3)
    total(0)
    total(1)
    pick(2)
    pick(3)
    settle(0)
    settle(1)
    total(2)
    total(3)
    settle(2)
    settle(3)

    @pl.when(me < 7)
    def _():
        @pl.loop(0, H)
        def _(h):
            pass_on(h).wait_send()

    copies.finish()


def chain(idx, m1, b1, bo, flag, f0):
    vm = pltpu.VMEM

    def units(*n):
        return vm(n + (D, D), F32)

    return pl.pallas_call(
        chain_kernel,
        out_shape=(
            jax.ShapeDtypeStruct((H, D, D), F32),
            jax.ShapeDtypeStruct((REQS, REQS, D, D), F32),
        ),
        in_specs=[SMEM, ANY, ANY, ANY, VMEM, ANY],
        out_specs=(VMEM, VMEM),
        scratch_shapes=[
            pltpu.SMEM((2, 16), jnp.int32),
            units(H), units(H), units(H), pltpu.SemaphoreType.DMA((16,)),
            units(H), units(8, 4, 4), units(4, 4, 4),
            units(4, 4), units(4, 4), units(4, 4),
            units(16), units(16), units(16), units(16), units(16, 4),
            units(4, 2), units(4, 2), units(4, 4), units(4, 4),
            pltpu.SemaphoreType.DMA((H,)),
            pltpu.SemaphoreType.DMA((H,)),
            pltpu.SemaphoreType.DMA((64,)),
            pltpu.SemaphoreType.DMA((64,)),
        ],
        compiler_params=pltpu.CompilerParams(
            collective_id=0, has_side_effects=True, vmem_limit_bytes=60 * 1024 * 1024
        ),
        name="state_chain",
    )(idx, m1, b1, bo, flag, f0)


HB = 8


def gate_kernel(out0_ref, qe_ref, x_ref, gate_ref, gain_ref, o_ref):
    gain = gain_ref[...]
    gate = gate_ref.reshape(TOK * HB, D)
    dst = o_ref.reshape(TOK * HB, D)
    for h in range(HB):
        raw = out0_ref[h] + dot_wide(qe_ref[h], x_ref[h])
        ms = jnp.sum(raw * raw, axis=1, keepdims=True) * (1.0 / D)
        g = gate[pl.ds(h, TOK, stride=HB), :]
        act = g / (1.0 + jnp.exp(-g))
        dst[pl.ds(h, TOK, stride=HB), :] = raw * lax.rsqrt(ms + 1e-6) * gain * act


def gated_out(out0, qe, x_in, gate, gain):
    tok = pl.BlockSpec((HB, TOK, D), lambda i: (i, 0, 0))
    nat = pl.BlockSpec((TOK, HB, D), lambda i: (0, i, 0))
    return pl.pallas_call(
        gate_kernel,
        grid=(H // HB,),
        out_shape=jax.ShapeDtypeStruct((TOK, H, D), F32),
        in_specs=[
            tok, tok,
            pl.BlockSpec((HB, D, D), lambda i: (i, 0, 0)),
            nat,
            pl.BlockSpec((1, D), lambda i: (0, 0)),
        ],
        out_specs=nat,
        compiler_params=pltpu.CompilerParams(vmem_limit_bytes=60 * 1024 * 1024),
        cost_estimate=pl.CostEstimate(flops=800000000, bytes_accessed=20000000, transcendentals=0),
        name="gated_out",
    )(out0, qe, x_in, gate, gain)


def local(
    queries, key_vecs, val_vecs, out_gate, log_decay, beta_gate, norm_gain, lengths, owner_slot
):
    out0, qe, m1, b1, bo, f0, flag = local_terms(
        lengths,
        queries.reshape(TOK * HK, D),
        key_vecs.reshape(TOK * HK, D),
        val_vecs.reshape(TOK * H, D),
        log_decay[0],
        beta_gate[0],
    )
    x_in, decode = chain(owner_slot, m1, b1, bo, flag, f0)
    attn = gated_out(out0, qe, x_in, out_gate[0], norm_gain.reshape(1, D))
    return attn[None], decode


def solution(mesh):
    return jax.shard_map(
        local,
        mesh=mesh,
        in_specs=(
            P("grp", "ctx", None, None),
            P("grp", "ctx", None, None),
            P("grp", "ctx", None, None),
            P("grp", "ctx", None, None),
            P("grp", None, "ctx"),
            P("grp", None, "ctx"),
            P(),
            P("grp", None),
            P(),
        ),
        out_specs=(P("grp", "ctx", None, None), P("grp", "ctx", None, None)),
        check_vma=False,
    )
```

time: 248 us -> 180 us (0.73); the launches traced: 244 us -> 180 us
  Pallas kernels: 230 us -> 178 us
  local copies, waits for them, and re-layouts: 10.9 us -> 0.97 us
    pallas_call x1, Pallas kernels: 150 us -> 115 us  [chain(): pl.pallas_call(chain_kernel, out_shape=(jax.ShapeDtypeStruct((H, D, D), F...]
    pallas_call x1, Pallas kernels: 73 us -> 54.1 us  [local_terms(): pl.pallas_call(terms_kernel, out_shape=(tokens, tokens, hm, hm, hm, jax.S...]
    unnamed x11 -> x3, local copies, waits for them, and re-layouts: 6.94 us -> 0.97 us
    pallas_call x1, Pallas kernels: 6.92 us -> 9.46 us  [gated_out(): pl.pallas_call(gate_kernel, grid=(H // HB,), out_shape=jax.ShapeDtypeStru...]
where the time goes in v2:
time: 180 us
  Pallas kernels  178 us (99%)
    pallas_call x1, Pallas kernels, chain(): pl.pallas_call(chain_kernel, out_shape=(jax.ShapeDtypeStruct((H, D, D), F...  115 us
    pallas_call x1, Pallas kernels, local_terms(): pl.pallas_call(terms_kernel, out_shape=(tokens, tokens, hm, hm, hm, jax.S...  54.1 us
    pallas_call x1, Pallas kernels, gated_out(): pl.pallas_call(gate_kernel, grid=(H // HB,), out_shape=jax.ShapeDtypeStru...  9.46 us

profile of v2, /device:TPU:5, one launch (start us, length us, event | category | flops | bytes accessed | tf_op | source)
XLA Modules:
  0.0 180.1 jit_solution(14091805862771433825)
XLA Ops:
  0.6 54.1 %local_terms.1 = (f32[32,256,128]{2,1,0:T(8,128)}, f32[32,256,128]{2,1,0:T(8,128)}, f32[32,128,128]{2,1,0:T(8,128)}, f32[32,128,128]{2,1,0:T(8,128)}, f32[32,128...) custom-call(s32[1,4]{1,0:T(1,128)} %len_ref.1, f32[4096,128]{1,0:T(8,128)} %bitcast.11, ...), custom_call_target="tpu_custom_call" | custom-call | tf_op jit(solution)/shard_map/local_terms/pallas_call | solution.py:298
  54.8 114.9 %state_chain.1 = (f32[32,128,128]{2,1,0:T(8,128)}, f32[4,4,128,128]{3,2,1,0:T(8,128)}) custom-call(s32[64]{0:T(128)} %own_ref.1, f32[32,128,128]{2,1,0:T(8,128)} %get-tuple-element.13.m_hbm, f32[32,128,128]{2,1,0:T(8,128)} %get-tuple-element.14.b1_hbm, f32[32,128,128]{2,1,0:T(8,128)} %get-tuple-element.15.bo_hbm, f32[8,128]{1,0:T(8,128)} %get-tuple-element.16.flag_ref, ...), custom_call_target="tpu_custom_call" | custom-call | tf_op jit(solution)/shard_map/state_chain/pallas_call | solution.py:603
  169.7 0.0 copy-start
  169.7 9.5 %gated_out.1 = f32[256,32,128]{2,1,0:T(8,128)} custom-call(f32[32,256,128]{2,1,0:T(8,128)} %get-tuple-element.11.out0_ref, f32[32,256,128]{2,1,0:T(8,128)} %get-tuple-element.12.qe_ref, f32[32,128,128]{2,1,0:T(8,128)} %get-tuple-element.18.x_ref, f32[256,32,128]{2,1,0:T(8,128)} %bitcast.9, f32[1,128]{1,0:T(1,128)} %bitcast.15), custom_call_target="tpu_custom_call" | custom-call | flops 800000000 | bytes 20000000 | tf_op jit(solution)/shard_map/gated_out/pallas_call | solution.py:648
  179.1 0.0 copy-done
  179.2 1.0 copy.12
Async XLA Ops:
  169.7 9.5 %copy-start = (f32[4,4,128,128]{3,2,1,0:T(8,128)S(1)}, f32[4,4,128,128]{3,2,1,0:T(8,128)}, u32[]{:S(2)}) copy-start(f32[4,4,128,128]{3,2,1,0:T(8,128)} %get-tuple-element.23) | copy-start | bytes 3145732

commit v3 on v2

--- a/solution.py
+++ b/solution.py
@@ -471,6 +471,12 @@
                 end_s[at, c, p] = end_s[at, c, p] + here * xt
 
     twins, back, ahead, last = [], [], [], []
+    span = pl.ds(chip // 2, 3)
+
+    def add_span(j, at, sender, src):
+        lo = sender // 2
+        for u in range(3):
+            twin_s[j, at, lo + u] = twin_s[j, at, lo + u] + src[j, lo + u]
 
     def join(j):
         twins[j].wait_recv()
@@ -479,11 +485,11 @@
         def _(c):
             add_units(twin_s.at[j], c, 0, 4, end_s.at[j * 2 + core, c])
 
-        back.append(copies.start(twin_s.at[j, x_opp], xb.at[j], x_down))
+        back.append(copies.start(twin_s.at[j, x_opp, span], xb.at[j, span], x_down))
 
     def relay(j):
         back[j].wait_recv()
-        add_units(twin_s.at[j], x_prev, 0, 4, xb.at[j])
+        add_span(j, x_prev, x_next, xb)
         last.append(copies.start(twin_s.at[j, x_prev], xd.at[j], x_down))
 
     for j in range(4):
@@ -493,12 +499,12 @@
         if j >= 1:
             join(j - 1)
     relay(0)
-    ahead.append(copies.start(twin_s.at[0, x_next], xc.at[0], x_up))
-    ahead.append(copies.start(twin_s.at[1, x_next], xc.at[1], x_up))
+    ahead.append(copies.start(twin_s.at[0, x_next, span], xc.at[0, span], x_up))
+    ahead.append(copies.start(twin_s.at[1, x_next, span], xc.at[1, span], x_up))
     join(3)
     relay(1)
-    ahead.append(copies.start(twin_s.at[2, x_next], xc.at[2], x_up))
-    ahead.append(copies.start(twin_s.at[3, x_next], xc.at[3], x_up))
+    ahead.append(copies.start(twin_s.at[2, x_next, span], xc.at[2, span], x_up))
+    ahead.append(copies.start(twin_s.at[3, x_next, span], xc.at[3, span], x_up))
 
     places = ((z, at["z"], y, at["y"]), (y, at["y"], z, at["z"]))
     direct, onward, begun, passed = [], [], [], []
@@ -507,8 +513,9 @@
         pos, (up, down), _, _ = places[j % 2]
         ahead[j].wait_recv()
         last[j].wait_recv()
+        add_span(j, chip, x_prev, xc)
         for u in range(4):
-            got_s[j][pos * 4 + u] = twin_s[j, chip, u] + xc[j, u] + xd[j, u]
+            got_s[j][pos * 4 + u] = twin_s[j, chip, u] + xd[j, u]
         mine = got_s[j].at[pl.ds(pos * 4, 4)]
         direct.append((copies.start(mine, mine, up), copies.start(mine, mine, down)))
 

time: 180 us -> 178 us (0.989)
  Pallas kernels: 178 us -> 176 us
    pallas_call x1, Pallas kernels: 115 us -> 113 us  [chain(): pl.pallas_call(chain_kernel, out_shape=(jax.ShapeDtypeStruct((H, D, D), F...]
where the time goes in v3:
time: 178 us
  Pallas kernels  176 us (99%)
    pallas_call x1, Pallas kernels, chain(): pl.pallas_call(chain_kernel, out_shape=(jax.ShapeDtypeStruct((H, D, D), F...  113 us
    pallas_call x1, Pallas kernels, local_terms(): pl.pallas_call(terms_kernel, out_shape=(tokens, tokens, hm, hm, hm, jax.S...  54.1 us
    pallas_call x1, Pallas kernels, gated_out(): pl.pallas_call(gate_kernel, grid=(H // HB,), out_shape=jax.ShapeDtypeStru...  9.46 us

profile of v3, /device:TPU:5, one launch (start us, length us, event | category | flops | bytes accessed | tf_op | source)
XLA Modules:
  0.0 178.0 jit_solution(12625709451626155320)
XLA Ops:
  0.6 54.1 %local_terms.1 = (f32[32,256,128]{2,1,0:T(8,128)}, f32[32,256,128]{2,1,0:T(8,128)}, f32[32,128,128]{2,1,0:T(8,128)}, f32[32,128,128]{2,1,0:T(8,128)}, f32[32,128...) custom-call(s32[1,4]{1,0:T(1,128)} %len_ref.1, f32[4096,128]{1,0:T(8,128)} %bitcast.11, ...), custom_call_target="tpu_custom_call" | custom-call | tf_op jit(solution)/shard_map/local_terms/pallas_call | solution.py:298
  54.8 112.8 %state_chain.1 = (f32[32,128,128]{2,1,0:T(8,128)}, f32[4,4,128,128]{3,2,1,0:T(8,128)}) custom-call(s32[64]{0:T(128)} %own_ref.1, f32[32,128,128]{2,1,0:T(8,128)} %get-tuple-element.13.m_hbm, f32[32,128,128]{2,1,0:T(8,128)} %get-tuple-element.14.b1_hbm, f32[32,128,128]{2,1,0:T(8,128)} %get-tuple-element.15.bo_hbm, f32[8,128]{1,0:T(8,128)} %get-tuple-element.16.flag_ref, ...), custom_call_target="tpu_custom_call" | custom-call | tf_op jit(solution)/shard_map/state_chain/pallas_call | solution.py:610
  167.6 0.0 copy-start
  167.6 9.5 %gated_out.1 = f32[256,32,128]{2,1,0:T(8,128)} custom-call(f32[32,256,128]{2,1,0:T(8,128)} %get-tuple-element.11.out0_ref, f32[32,256,128]{2,1,0:T(8,128)} %get-tuple-element.12.qe_ref, f32[32,128,128]{2,1,0:T(8,128)} %get-tuple-element.18.x_ref, f32[256,32,128]{2,1,0:T(8,128)} %bitcast.9, f32[1,128]{1,0:T(1,128)} %bitcast.15), custom_call_target="tpu_custom_call" | custom-call | flops 800000000 | bytes 20000000 | tf_op jit(solution)/shard_map/gated_out/pallas_call | solution.py:655
  177.0 0.0 copy-done
  177.0 1.0 copy.12
Async XLA Ops:
  167.6 9.5 %copy-start = (f32[4,4,128,128]{3,2,1,0:T(8,128)S(1)}, f32[4,4,128,128]{3,2,1,0:T(8,128)}, u32[]{:S(2)}) copy-start(f32[4,4,128,128]{3,2,1,0:T(8,128)} %get-tuple-element.23) | copy-start | bytes 3145732
